TPU v7x, 512 devices: a whole 4x4x16 slice. The times are simulated.
512 devices in a mesh: grp: 8 (over x, z_hi), blk: 64 (over z_lo, y, core).
Axes of the slice: x: 4, y: 4, z: 16 (z_hi: 2, z_lo: 8; z = z_hi * 8 + z_lo), core: 2. Of those that a mesh axis runs over, the one named last changes fastest.
Arguments:
- grad: bfloat16 [320, 16384], P(None, ('grp', 'blk')), may hold values from -6 to 6
- moment: float32 [320, 16384], P(None, ('grp', 'blk')), may hold values from -4 to 4
- second_moment: float32 [320, 16384], P('grp', 'blk'), may hold values from 0.01 to 1
- left_basis: bfloat16 [320, 320], replicated, may hold values from -0.3125 to 0.3125
- right_basis: bfloat16 [16384, 16384], P('grp', 'blk'), may hold values from -0.046875 to 0.046875
Outputs:
- momentum: float32 [320, 16384], P(None, ('grp', 'blk'))
- second: float32 [320, 16384], P('grp', 'blk')
- update: float32 [320, 16384], P(None, ('grp', 'blk'))
All inputs are finite; a program needn't handle non-finite values.
Results may differ from a plain program's by a relative error of at most 0.0049.
Values may be sent and summed in bfloat16 or wider, within the bound.
No kernel may reach another device: no remote copies, remote signals or barrier semaphores. Data moves between devices by JAX's collectives and lax.ppermute only.
A program may use at most 64 MiB of HBM per device.

v0:
```python
import jax
import jax.numpy as jnp
from jax import lax
from jax.sharding import PartitionSpec as P

beta_first = 0.95
beta_second = 0.95
epsilon_root = 1e-08


def left_rotate(values, left_basis):
    return lax.dot_general(
        values, left_basis, (((0,), (0,)), ((), ())), preferred_element_type=jnp.float32
    ).astype(jnp.bfloat16)


def per_device(grad, moment, second_moment, left_basis, right_basis):
    momentum = beta_first * moment + (1.0 - beta_first) * grad.astype(jnp.float32)
    momentum_bf = momentum.astype(jnp.bfloat16)
    left_grad = left_rotate(grad, left_basis)
    left_moment = left_rotate(momentum_bf, left_basis)

    def rotate(piece):
        return lax.dot_general(
            piece,
            right_basis,
            (((piece.ndim - 2,), (0,)), ((), ())),
            preferred_element_type=jnp.float32,
        )

    grad_part = rotate(lax.all_gather(left_grad, "blk", axis=0, tiled=True))
    moment_part = rotate(lax.all_gather(left_moment, "blk", axis=0, tiled=True))
    partial_value = jnp.stack([grad_part, moment_part])
    summed = lax.psum_scatter(partial_value, "grp", scatter_dimension=1, tiled=True)
    second = beta_second * second_moment + (1.0 - beta_second) * summed[0] * summed[0]
    direction = (summed[1] / (jnp.sqrt(second) + epsilon_root)).astype(jnp.bfloat16)
    full_direction = lax.all_gather(direction, "grp", axis=0, tiled=True)
    back_t = lax.psum_scatter(
        lax.dot_general(
            right_basis,
            full_direction,
            (((1,), (1,)), ((), ())),
            preferred_element_type=jnp.float32,
        ),
        "blk",
        scatter_dimension=0,
        tiled=True,
    ).astype(jnp.bfloat16)
    update_t = lax.dot_general(
        back_t, left_basis, (((1,), (1,)), ((), ())), preferred_element_type=jnp.float32
    )
    return (momentum, second, update_t.T)


def solution(mesh):
    in_specs = (
        P(None, ("grp", "blk")),
        P(None, ("grp", "blk")),
        P("grp", "blk"),
        P(),
        P("grp", "blk"),
    )
    out_specs = (P(None, ("grp", "blk")), P("grp", "blk"), P(None, ("grp", "blk")))
    return jax.shard_map(
        per_device, mesh=mesh, in_specs=in_specs, out_specs=out_specs, check_vma=False
    )
```

profile of v0, /device:TPU:6, one launch (start us, length us, event | category | flops | bytes accessed | tf_op | source)
XLA Modules:
  0.0 878.5 jit_solution(6904321276063047940)
XLA Ops:
  7.2 0.0 copy-start
  7.2 0.0 all-gather.3.cloned.1.call-start
  7.2 1.8 convolution_convert_fusion.1
  9.0 0.0 all-gather.3.cloned.1.call-update
  9.1 0.0 all-gather.5.cloned.1.call-start
  9.1 0.8 multiply_add_fusion
  9.9 0.0 copy-start.2
  10.0 1.7 convolution_convert_fusion
  11.7 0.0 all-gather.5.cloned.1.call-update
  11.7 0.0 reduce-scatter.5.cloned.1.call-start
  11.8 123.8 %all-gather.3.cloned.1.call-done = bf16[2048,320]{1,0:T(8,128)(2,1)} async-done(((bf16[32,320]{1,0:T(8,128)(2,1)}), bf16[2048,320]{1,0:T(8,128)(2,1)}) %all-gather.3.cloned.1.call-update) | async-done | bytes 1310736 | tf_op jit(solution)/shard_map/all_gather | solution.py:31
  135.6 0.0 copy-done
  135.6 2.0 convolution_bitcast_fusion.2
  137.6 0.0 copy-done.2
  137.6 116.9 %all-gather.5.cloned.1.call-done = bf16[2048,320]{1,0:T(8,128)(2,1)} async-done(((bf16[32,320]{1,0:T(8,128)(2,1)}), bf16[2048,320]{1,0:T(8,128)(2,1)}) %all-gather.5.cloned.1.call-update) | async-done | bytes 1310736 | tf_op jit(solution)/shard_map/all_gather | solution.py:32
  254.6 2.0 convolution_bitcast_fusion.1
  256.6 0.0 copy-start.3
  256.6 0.9 pad_maximum_fusion
  257.5 0.0 reduce-scatter.5.cloned.1.call-update
  257.5 0.0 reduce-scatter.7.cloned.1.call-start
  257.5 111.2 %reduce-scatter.5.cloned.1.call-done = f32[2,40,256]{2,1,0:T(8,128)} async-done(((f32[2,320,256]{2,1,0:T(8,128)}), f32[2,40,256]{2,1,0:T(8,128)}) %reduce-scatter.5.cloned.1.call-update) | async-done | bytes 81936 | tf_op jit(solution)/shard_map/reduce_scatter | solution.py:34
  368.8 0.0 copy-done.3
  368.8 1.4 fusion.3
  370.2 62.0 %all_gather.11 = bf16[320,256]{1,0:T(8,128)(2,1)S(1)} all-gather(bf16[40,256]{1,0:T(8,128)(2,1)S(1)} %get-tuple-element.3), channel_id=1, replica_groups=mesh['grp'=8,'blk'=64] {'grp'}, dimensions={0}, use_global_device_ids=true | all-gather | bytes 184320 | tf_op jit(solution)/shard_map/all_gather | solution.py:37
  432.2 2.1 convolution_bitcast_fusion
  434.3 3.4 copy.8
  437.7 0.0 copy-start.1
  437.7 0.0 reduce-scatter.7.cloned.1.call-update
  437.7 432.5 %reduce-scatter.7.cloned.1.call-done = f32[32,320]{1,0:T(8,128)} async-done(((f32[2048,320]{1,0:T(8,128)}), f32[32,320]{1,0:T(8,128)}) %reduce-scatter.7.cloned.1.call-update) | async-done | bytes 40976
  870.2 0.9 copy.9
  871.1 0.0 copy-done.1
  871.1 0.8 convolution_bitcast_fusion.3
Async XLA Ops:
  7.2 128.4 %copy-start = (bf16[2048,256]{1,0:T(8,128)(2,1)S(1)}, bf16[2048,256]{1,0:T(8,128)(2,1)}, u32[]{:S(2)}) copy-start(bf16[2048,256]{1,0:T(8,128)(2,1)} %param.9) | copy-start | bytes 3145732
  7.2 128.4 %all-gather.3.cloned.1.call-start = ((), (), s32[]{:S(2)}) async-start(), calls=%async_computation.2 | async-start | bytes 1597440 | tf_op jit(solution)/shard_map/all_gather | solution.py:31
  9.1 245.5 %all-gather.5.cloned.1.call-start = ((), (), s32[]{:S(2)}) async-start(), calls=%async_computation.3 | async-start | bytes 1597440 | tf_op jit(solution)/shard_map/all_gather | solution.py:32
  9.9 127.7 %copy-start.2 = (f32[320,32]{0,1:T(8,128)}, f32[320,32]{0,1:T(8,128)S(1)}, u32[]{:S(2)}) copy-start(f32[320,32]{0,1:T(8,128)S(1)} %multiply_add_fusion) | copy-start | bytes 122884
  11.7 357.1 %reduce-scatter.5.cloned.1.call-start = ((), (), s32[]{:S(2)}) async-start(), calls=%async_computation.4 | async-start | bytes 737280 | tf_op jit(solution)/shard_map/reduce_scatter | solution.py:34
  256.6 112.2 %copy-start.3 = (f32[40,256]{1,0:T(8,128)S(1)}, f32[40,256]{1,0:T(8,128)}, u32[]{:S(2)}) copy-start(f32[40,256]{1,0:T(8,128)} %param.7) | copy-start | bytes 122884
  257.5 612.7 %reduce-scatter.7.cloned.1.call-start = ((), (), s32[]{:S(2)}) async-start(), calls=%async_computation.5 | async-start | bytes 3194880
  437.7 433.4 %copy-start.1 = (bf16[320,320]{1,0:T(8,128)(2,1)S(1)}, bf16[320,320]{1,0:T(8,128)(2,1)}, u32[]{:S(2)}) copy-start(bf16[320,320]{1,0:T(8,128)(2,1)} %param.8) | copy-start | bytes 614404
Sparse Core Ops, SparseCore 0:
  10.7 124.8 all-gather.2
  138.3 116.1 all-gather.4
  259.0 109.6 reduce-scatter.4
  437.8 432.2 reduce-scatter.6
where the time goes:
time: 879 us; the launch traced here: 878 us
  waiting for transfers between devices  785 us (89%)
  blocking collectives  62 us (7%)
  between operations  13.8 us (2%)
  matrix products  10.4 us (1%)
    unnamed x5, waiting for transfers between devices  433 us
    all_gather x1, waiting for transfers between devices, per_device(): grad_part = rotate(lax.all_gather(left_grad, 'blk', axis=0, tiled=True))  124 us
    all_gather x1, waiting for transfers between devices, per_device(): moment_part = rotate(lax.all_gather(left_moment, 'blk', axis=0, tiled=True))  117 us
    reduce_scatter x1, waiting for transfers between devices, per_device(): lax.psum_scatter(partial_value, 'grp', scatter_dimension=1, tiled=True)  111 us
    all_gather x1, blocking collectives, per_device(): full_direction = lax.all_gather(direction, 'grp', axis=0, tiled=True)  62 us
  transfers between devices with their start and end apart: 4, of which 4 were waited for; matrix products, arithmetic and copies ran while one was open for 1% of the time, Pallas kernels for 0%

commit v1 on v0

v1 whole, which is shorter than its diff:
```python
import jax
import jax.numpy as jnp
from jax import lax
from jax.sharding import Mesh, PartitionSpec as P

beta_first = 0.95
beta_second = 0.95
epsilon_root = 1e-08

f32 = jnp.float32
bf16 = jnp.bfloat16
X, ZH, ZL, Y, C = 4, 2, 8, 4, 2
SWAP = [(0, 1), (1, 0)]


def left_rotate(values, left_basis):
    return lax.dot_general(
        values, left_basis, (((0,), (0,)), ((), ())), preferred_element_type=f32
    ).astype(bf16)


def spread(values, axis, count):
    return lax.all_to_all(
        jnp.broadcast_to(values[None], (count,) + values.shape), axis, 0, 0
    )


def add_up(values):
    return jnp.sum(values.astype(f32), axis=0)


def per_device(grad, moment, second_moment, left_basis, right_basis):
    core = lax.axis_index("core")
    momentum = beta_first * moment + (1.0 - beta_first) * grad.astype(f32)
    left = jnp.concatenate(
        [left_rotate(grad, left_basis), left_rotate(momentum.astype(bf16), left_basis)], axis=1
    )
    by_core = right_basis.reshape(ZL, Y, C, 32, 256)

    def rows_of(which):
        part = lax.dynamic_index_in_dim(by_core, which, 2, keepdims=False)
        return part.transpose(1, 0, 2, 3).reshape(1024, 256)

    right_own, right_other = rows_of(core), rows_of(1 - core)

    left = spread(left, "zl", ZL)
    left = spread(left.reshape(256, 640), "y", Y).reshape(1024, 640)
    left_other = lax.ppermute(left, "core", SWAP)

    def rotate(piece, basis):
        return lax.dot_general(piece, basis, (((0,), (0,)), ((), ())), preferred_element_type=f32)

    part = rotate(left, right_own) + rotate(left_other, right_other)
    part = part.reshape(2, 8, 40, 256).transpose(1, 0, 2, 3).astype(bf16)
    summed = add_up(lax.all_to_all(part, ("x", "zh"), 0, 0))
    second = beta_second * second_moment + (1.0 - beta_second) * summed[0] * summed[0]
    direction = (summed[1] / (jnp.sqrt(second) + epsilon_root)).astype(bf16)
    direction = spread(direction, ("x", "zh"), X * ZH).reshape(320, 256)

    def back_rotate(basis):
        return lax.dot_general(
            basis, direction, (((1,), (1,)), ((), ())), preferred_element_type=f32
        )

    sent = lax.ppermute(back_rotate(right_other).astype(bf16), "core", SWAP)
    back = back_rotate(right_own) + sent.astype(f32)
    back = lax.all_to_all(back.astype(bf16).reshape(Y, ZL * 32, 320), "y", 0, 0)
    back = add_up(back).astype(bf16).reshape(ZL, 32, 320)
    back = add_up(lax.all_to_all(back, "zl", 0, 0)).astype(bf16)
    update = lax.dot_general(
        left_basis, back, (((1,), (1,)), ((), ())), preferred_element_type=f32
    )
    return (momentum, second, update)


def solution(mesh):
    names = ("x", "zh", "zl", "y", "core")
    fine = Mesh(mesh.devices.reshape(X, ZH, ZL, Y, C), names)
    columns = P(None, names)
    block = P(("x", "zh"), ("zl", "y", "core"))
    return jax.shard_map(
        per_device,
        mesh=fine,
        in_specs=(columns, columns, block, P(), block),
        out_specs=(columns, block, columns),
        check_vma=False,
    )
```

time: 879 us -> 158 us (0.18)
  waiting for transfers between devices: 785 us -> 4.44 us
  blocking collectives: 62 us -> 138 us
  between operations: 13.8 us -> 0.82 us
    unnamed x5 -> x0, waiting for transfers between devices: 433 us -> none
    all_gather x2 -> x0, waiting for transfers between devices: 241 us -> none  [the longest x1 124 us: per_device(): grad_part = rotate(lax.all_gather(left_grad, 'blk', axis=0, tiled=True))]
    all_to_all x0 -> x6, blocking collectives: none -> 138 us  [the longest x3 69.6 us: spread(): lax.all_to_all(jnp.broadcast_to(values[None], (count,) + values.shape), a...]
    reduce_scatter x1 -> x0, waiting for transfers between devices: 111 us -> none  [per_device(): lax.psum_scatter(partial_value, 'grp', scatter_dimension=1, tiled=True)]
    all_gather x1 -> x0, blocking collectives: 62 us -> none  [per_device(): full_direction = lax.all_gather(direction, 'grp', axis=0, tiled=True)]
  transfers between devices with their start and end apart: 4 -> 2, of which waited for: 4 -> 2; matrix products, arithmetic and copies ran while one was open for 1% -> 0% of each run, Pallas kernels for 0% -> 0%
where the time goes in v1:
time: 158 us; the launch traced here: 156 us
  blocking collectives  138 us (87%)
  matrix products  4.99 us (3%)
  waiting for transfers between devices  4.44 us (3%)
  starting transfers between devices  3.83 us (2%)
  other arithmetic  1.74 us (1%)
    all_to_all x3, blocking collectives, spread(): lax.all_to_all(jnp.broadcast_to(values[None], (count,) + values.shape), a...  69.6 us
    all_to_all x1, blocking collectives, per_device(): back = add_up(lax.all_to_all(back, 'zl', 0, 0)).astype(bf16)  29.1 us
    all_to_all x1, blocking collectives, per_device(): summed = add_up(lax.all_to_all(part, ('x', 'zh'), 0, 0))  25.8 us
    all_to_all x1, blocking collectives, per_device(): back = lax.all_to_all(back.astype(bf16).reshape(Y, ZL * 32, 320), 'y', 0, 0)  13.9 us
  transfers between devices with their start and end apart: 2, of which 2 were waited for; matrix products, arithmetic and copies ran while one was open for 0% of the time, Pallas kernels for 0%

profile of v1, /device:TPU:6, one launch (start us, length us, event | category | flops | bytes accessed | tf_op | source)
XLA Modules:
  0.0 155.6 jit_solution(17296000954347422635)
XLA Ops:
  0.6 0.0 copy-start
  0.6 0.9 copy-done
  1.6 0.9 convolution_convert_fusion.2
  2.5 0.8 multiply_add_fusion
  3.3 0.0 copy-start.2
  3.3 0.2 convolution_convert_fusion.1
  3.5 0.1 pad_maximum_fusion
  3.6 32.4 %all_to_all.30 = bf16[8,32,640]{2,1,0:T(8,128)(2,1)S(1)} all-to-all(bf16[8,32,640]{2,1,0:T(8,128)(2,1)S(1)} %broadcast_in_dim.8), channel_id=1, replica_groups=mesh['x'=4,'zh'=2,'zl'=8,'y'=4,'core'=2] {'zl'}, dimensions={0} | all-to-all | bytes 655360 | tf_op jit(solution)/shard_map/all_to_all | solution.py:23
  36.0 0.1 broadcast_in_dim.10
  36.1 0.0 copy-done.2
  36.1 0.0 copy-start.1
  36.1 19.4 %all_to_all.31 = bf16[4,256,640]{2,1,0:T(8,128)(2,1)S(1)} all-to-all(bf16[4,256,640]{2,1,0:T(8,128)(2,1)S(1)} %broadcast_in_dim.10), channel_id=1, replica_groups=mesh['x'=4,'zh'=2,'zl'=8,'y'=4,'core'=2] {'y'}, dimensions={0} | all-to-all | bytes 2621440 | tf_op jit(solution)/shard_map/all_to_all | solution.py:23
  55.6 1.9 %collective-permute-start = (bf16[1024,640]{1,0:T(8,128)(2,1)S(1)}, bf16[1024,640]{1,0:T(8,128)(2,1)}, u32[]{:S(2)}, u32[]{:S(2)}) collective-permute-start(bf16[1024,640]{1,0:T(8,128)(2,1)S(1)} %bitcast.57), channel_id=1, source_target_pairs={{0,1},{1,0},{2,3},{3,2},{4,5},{5,4},{6,7},{7,6},{8,9},{9,8},{10,11... | collective-permute-start | bytes 3932168 | tf_op jit(solution)/shard_map/ppermute | solution.py:48
  57.5 0.0 copy-done.1
  57.5 0.1 constant_dynamic-slice_fusion
  57.7 0.5 fusion.6
  58.2 2.4 %collective-permute-done = bf16[1024,640]{1,0:T(8,128)(2,1)} collective-permute-done((bf16[1024,640]{1,0:T(8,128)(2,1)S(1)}, bf16[1024,640]{1,0:T(8,128)(2,1)}, u32[]{:S(2)}, u32[]{:S(2)}) %collective-permute-start) | collective-permute-done | bytes 1310752 | tf_op jit(solution)/shard_map/ppermute | solution.py:48
  60.6 1.9 %fusion = bf16[640,256]{1,0:T(8,128)(2,1)S(1)} fusion(f32[640,256]{1,0:T(8,128)S(1)} %fusion.6, bf16[1024,640]{1,0:T(8,128)(2,1)} %collective-permute-done, bf16[1024,256]{1,0:T(8,128)(2,1)S(1)} %bitcast.53), kind=kOutput, calls=%fused_computation.3 | convolution fusion | flops 335872000 | bytes 2818048 | tf_op jit(solution)/shard_map/dot_general | solution.py:51
  62.5 0.0 copy-start.3
  62.5 25.8 %all_to_all.32 = bf16[8,2,40,256]{3,2,1,0:T(8,128)(2,1)S(1)} all-to-all(bf16[8,2,40,256]{3,2,1,0:T(8,128)(2,1)S(1)} %bitcast.59), channel_id=1, replica_groups=mesh['x'=4,'zh'=2,'zl'=8,'y'=4,'core'=2] {'x','zh'}, dimensions={0} | all-to-all | bytes 655360 | tf_op jit(solution)/shard_map/all_to_all | solution.py:55
  88.3 0.0 copy-done.3
  88.4 0.6 fusion.3
  89.0 17.7 %all_to_all.33 = bf16[8,40,256]{2,1,0:T(8,128)(2,1)S(1)} all-to-all(bf16[8,40,256]{2,1,0:T(8,128)(2,1)S(1)} %broadcast_in_dim.22), channel_id=1, replica_groups=mesh['x'=4,'zh'=2,'zl'=8,'y'=4,'core'=2] {'x','zh'}, dimensions={0} | all-to-all | bytes 327680 | tf_op jit(solution)/shard_map/all_to_all | solution.py:23
  106.7 0.4 convolution_convert_fusion
  107.1 1.9 %collective-permute-start.1 = (bf16[1024,320]{0,1:T(8,128)(2,1)S(1)}, bf16[1024,320]{0,1:T(8,128)(2,1)S(1)}, u32[]{:S(2)}, u32[]{:S(2)}) collective-permute-start(bf16[1024,320]{0,1:T(8,128)(2,1)S(1)} %convolution_convert_fusion), channel_id=1, source_target_pairs={{0,1},{1,0},{2,3},{3,2},{4,5},{5,4},{6,7},{7,6},{8,9},{9,8},{10,11... | collective-permute-start | bytes 1966088 | tf_op jit(solution)/shard_map/ppermute | solution.py:65
  109.0 2.1 %collective-permute-done.1 = bf16[1024,320]{0,1:T(8,128)(2,1)S(1)} collective-permute-done((bf16[1024,320]{0,1:T(8,128)(2,1)S(1)}, bf16[1024,320]{0,1:T(8,128)(2,1)S(1)}, u32[]{:S(2)}, u32[]{:S(2)}) %collective-permute-start.1) | collective-permute-done | bytes 655392 | tf_op jit(solution)/shard_map/ppermute | solution.py:65
  111.1 0.4 add_convert_fusion
  111.5 13.9 %all_to_all.34 = bf16[4,256,320]{1,2,0:T(8,128)(2,1)S(1)} all-to-all(bf16[4,256,320]{1,2,0:T(8,128)(2,1)S(1)} %bitcast.50), channel_id=1, replica_groups=mesh['x'=4,'zh'=2,'zl'=8,'y'=4,'core'=2] {'y'}, dimensions={0} | all-to-all | bytes 1310720 | tf_op jit(solution)/shard_map/all_to_all | solution.py:67
  125.4 0.1 reduce_sum.34
  125.5 0.2 copy.20
  125.7 29.1 %all_to_all.35 = bf16[8,32,320]{2,1,0:T(8,128)(2,1)S(1)} all-to-all(bf16[8,32,320]{2,1,0:T(8,128)(2,1)S(1)} %bitcast.62), channel_id=1, replica_groups=mesh['x'=4,'zh'=2,'zl'=8,'y'=4,'core'=2] {'zl'}, dimensions={0} | all-to-all | bytes 327680 | tf_op jit(solution)/shard_map/all_to_all | solution.py:69
  154.8 0.8 convolution_bitcast_fusion
  (8 shorter events, 0.3 us)
Async XLA Ops:
  0.6 1.0 copy-start
  3.3 32.8 %copy-start.2 = (f32[320,32]{0,1:T(8,128)}, f32[320,32]{0,1:T(8,128)S(1)}, u32[]{:S(2)}) copy-start(f32[320,32]{0,1:T(8,128)S(1)} %multiply_add_fusion) | copy-start | bytes 122884
  36.1 21.4 %copy-start.1 = (bf16[2048,256]{1,0:T(8,128)(2,1)S(1)}, bf16[2048,256]{1,0:T(8,128)(2,1)}, u32[]{:S(2)}) copy-start(bf16[2048,256]{1,0:T(8,128)(2,1)} %param.9) | copy-start | bytes 3145732
  55.6 5.0 %collective-permute-start = (bf16[1024,640]{1,0:T(8,128)(2,1)S(1)}, bf16[1024,640]{1,0:T(8,128)(2,1)}, u32[]{:S(2)}, u32[]{:S(2)}) collective-permute-start(bf16[1024,640]{1,0:T(8,128)(2,1)S(1)} %bitcast.57), channel_id=1, source_target_pairs={{0,1},{1,0},{2,3},{3,2},{4,5},{5,4},{6,7},{7,6},{8,9},{9,8},{10,11... | collective-permute-start | bytes 3932168 | tf_op jit(solution)/shard_map/ppermute | solution.py:48
  62.5 25.9 %copy-start.3 = (f32[40,256]{1,0:T(8,128)S(1)}, f32[40,256]{1,0:T(8,128)}, u32[]{:S(2)}) copy-start(f32[40,256]{1,0:T(8,128)} %param.7) | copy-start | bytes 122884
  107.1 4.0 %collective-permute-start.1 = (bf16[1024,320]{0,1:T(8,128)(2,1)S(1)}, bf16[1024,320]{0,1:T(8,128)(2,1)S(1)}, u32[]{:S(2)}, u32[]{:S(2)}) collective-permute-start(bf16[1024,320]{0,1:T(8,128)(2,1)S(1)} %convolution_convert_fusion), channel_id=1, source_target_pairs={{0,1},{1,0},{2,3},{3,2},{4,5},{5,4},{6,7},{7,6},{8,9},{9,8},{10,11... | collective-permute-start | bytes 1966088 | tf_op jit(solution)/shard_map/ppermute | solution.py:65

commit v2 on v1

v2 whole, which is shorter than its diff:
```python
import jax
import jax.numpy as jnp
from jax import lax
from jax.sharding import Mesh, PartitionSpec as P

beta_first = 0.95
beta_second = 0.95
epsilon_root = 1e-08

f32 = jnp.float32
bf16 = jnp.bfloat16
X, ZH, ZA, ZB, Y, C = 4, 2, 4, 2, 4, 2
SWAP = [(0, 1), (1, 0)]


def left_rotate(values, left_basis):
    return lax.dot_general(
        values, left_basis, (((0,), (0,)), ((), ())), preferred_element_type=f32
    ).astype(bf16)


def spread(values, axis, count):
    return lax.all_to_all(
        jnp.broadcast_to(values[None], (count,) + values.shape), axis, 0, 0
    )


def add_up(values):
    return jnp.sum(values.astype(f32), axis=0)


def per_device(grad, moment, second_moment, left_basis, right_basis):
    core = lax.axis_index("core")
    half = lax.axis_index("zh")
    momentum = beta_first * moment + (1.0 - beta_first) * grad.astype(f32)
    left = jnp.concatenate(
        [left_rotate(grad, left_basis), left_rotate(momentum.astype(bf16), left_basis)], axis=1
    )
    by_core = right_basis.reshape(ZA, ZB * Y, C, 32, 256)

    def rows_of(which):
        part = lax.dynamic_index_in_dim(by_core, which, 2, keepdims=False)
        return part.transpose(1, 0, 2, 3).reshape(1024, 256)

    right_own, right_other = rows_of(core), rows_of(1 - core)

    left = spread(left, "za", ZA)
    left = spread(left.reshape(128, 640), ("zb", "y"), ZB * Y).reshape(1024, 640)
    left_other = lax.ppermute(left, "core", SWAP)

    def rotate(piece, basis):
        return lax.dot_general(piece, basis, (((0,), (0,)), ((), ())), preferred_element_type=f32)

    part = rotate(left, right_own) + rotate(left_other, right_other)
    part = part.reshape(2, X, 80, 256).transpose(1, 0, 2, 3).astype(bf16)
    part = add_up(lax.all_to_all(part, "x", 0, 0))
    other = lax.ppermute(
        jnp.concatenate([part.reshape(160, 256), second_moment]).astype(bf16), "zh", SWAP
    ).astype(f32)
    summed = (part + other[:160].reshape(2, 80, 256)).reshape(2, ZH, 40, 256)
    mine = jnp.arange(ZH)[:, None, None] == half
    second_moments = jnp.where(mine, second_moment[None], other[None, 160:])
    second = beta_second * second_moments + (1.0 - beta_second) * summed[0] * summed[0]
    direction = (summed[1] / (jnp.sqrt(second) + epsilon_root)).astype(bf16)
    second = lax.dynamic_index_in_dim(second, half, 0, keepdims=False)
    direction = spread(direction.reshape(80, 256), "x", X).reshape(320, 256)

    def back_rotate(basis):
        return lax.dot_general(
            basis, direction, (((1,), (1,)), ((), ())), preferred_element_type=f32
        )

    sent = lax.ppermute(back_rotate(right_other).astype(bf16), "core", SWAP)
    back = back_rotate(right_own) + sent.astype(f32)
    back = lax.all_to_all(back.astype(bf16).reshape(ZB * Y, ZA * 32, 320), ("zb", "y"), 0, 0)
    back = add_up(back).astype(bf16).reshape(ZA, 32, 320)
    back = add_up(lax.all_to_all(back, "za", 0, 0)).astype(bf16)
    update = lax.dot_general(
        left_basis, back, (((1,), (1,)), ((), ())), preferred_element_type=f32
    )
    return (momentum, second, update)


def solution(mesh):
    names = ("x", "zh", "za", "zb", "y", "core")
    fine = Mesh(mesh.devices.reshape(X, ZH, ZA, ZB, Y, C), names)
    columns = P(None, names)
    block = P(("x", "zh"), ("za", "zb", "y", "core"))
    return jax.shard_map(
        per_device,
        mesh=fine,
        in_specs=(columns, columns, block, P(), block),
        out_specs=(columns, block, columns),
        check_vma=False,
    )
```

time: 158 us -> 136 us (0.86)
  blocking collectives: 138 us -> 73.4 us
  starting transfers between devices: 3.83 us -> 26.1 us
  waiting for transfers between devices: 4.44 us -> 24 us
    all_to_all x3 -> x1, blocking collectives: 68.7 us -> 19.4 us  [per_device(): lax.all_to_all(back.astype(bf16).reshape(ZB * Y, ZA * 32, 320), ('zb', 'y...]
    all_to_all x3, blocking collectives: 69.6 us -> 54 us  [spread(): lax.all_to_all(jnp.broadcast_to(values[None], (count,) + values.shape), a...]
    all_to_all x0 -> x2, waiting for transfers between devices: none -> 14.3 us  [the longest x1 8.67 us: per_device(): back = add_up(lax.all_to_all(back, 'za', 0, 0)).astype(bf16)]
    all_to_all x0 -> x2, starting transfers between devices: none -> 12.5 us  [the longest x1 7.72 us: per_device(): back = add_up(lax.all_to_all(back, 'za', 0, 0)).astype(bf16)]
    ppermute x0 -> x1, starting transfers between devices: none -> 9.78 us  [per_device(): lax.ppermute(jnp.concatenate([part.reshape(160, 256), second_moment]).ast...]
    ppermute x0 -> x1, waiting for transfers between devices: none -> 5.32 us  [per_device(): lax.ppermute(jnp.concatenate([part.reshape(160, 256), second_moment]).ast...]
  transfers between devices with their start and end apart: 2 -> 5, of which waited for: 2 -> 5; matrix products, arithmetic and copies ran while one was open for 0% -> 2% of each run, Pallas kernels for 0% -> 0%
where the time goes in v2:
time: 136 us; the launch traced here: 135 us
  blocking collectives  73.4 us (54%)
  starting transfers between devices  26.1 us (19%)
  waiting for transfers between devices  24 us (18%)
  matrix products  5 us (4%)
  local copies, waits for them, and re-layouts  2.8 us (2%)
  other arithmetic  2.56 us (2%)
    all_to_all x3, blocking collectives, spread(): lax.all_to_all(jnp.broadcast_to(values[None], (count,) + values.shape), a...  54 us
    all_to_all x1, blocking collectives, per_device(): lax.all_to_all(back.astype(bf16).reshape(ZB * Y, ZA * 32, 320), ('zb', 'y...  19.4 us
    ppermute x1, starting transfers between devices, per_device(): lax.ppermute(jnp.concatenate([part.reshape(160, 256), second_moment]).ast...  9.78 us
    all_to_all x1, waiting for transfers between devices, per_device(): back = add_up(lax.all_to_all(back, 'za', 0, 0)).astype(bf16)  8.67 us
    all_to_all x1, starting transfers between devices, per_device(): back = add_up(lax.all_to_all(back, 'za', 0, 0)).astype(bf16)  7.72 us
    all_to_all x1, waiting for transfers between devices, per_device(): part = add_up(lax.all_to_all(part, 'x', 0, 0))  5.59 us
    ppermute x1, waiting for transfers between devices, per_device(): lax.ppermute(jnp.concatenate([part.reshape(160, 256), second_moment]).ast...  5.32 us
    all_to_all x1, starting transfers between devices, per_device(): part = add_up(lax.all_to_all(part, 'x', 0, 0))  4.77 us
  transfers between devices with their start and end apart: 5, of which 5 were waited for; matrix products, arithmetic and copies ran while one was open for 2% of the time, Pallas kernels for 0%

profile of v2, /device:TPU:6, one launch (start us, length us, event | category | flops | bytes accessed | tf_op | source)
XLA Modules:
  0.0 134.8 jit_solution(7527635433364868304)
XLA Ops:
  0.6 0.0 copy-start
  0.6 0.9 multiply_add_fusion
  1.5 0.1 copy-done
  1.6 0.0 copy-start.3
  1.6 0.9 convolution_convert_fusion.2
  2.5 0.2 convolution_convert_fusion.1
  2.7 0.1 pad_maximum_fusion.1
  2.8 24.2 %all_to_all.30 = bf16[4,32,640]{2,1,0:T(8,128)(2,1)S(1)} all-to-all(bf16[4,32,640]{2,1,0:T(8,128)(2,1)S(1)} %broadcast_in_dim.59), channel_id=1, replica_groups=mesh['x'=4,'zh'=2,'za'=4,'zb'=2,'y'=4,'core'=2] {'za'}, dimensions={0} | all-to-all | bytes 327680 | tf_op jit(solution)/shard_map/all_to_all | solution.py:23
  27.0 0.1 broadcast_in_dim.61
  27.2 0.0 copy-done.3
  27.2 0.0 copy-start.1
  27.2 21.3 %all_to_all.31 = bf16[8,128,640]{2,1,0:T(8,128)(2,1)S(1)} all-to-all(bf16[8,128,640]{2,1,0:T(8,128)(2,1)S(1)} %broadcast_in_dim.61), channel_id=1, replica_groups=mesh['x'=4,'zh'=2,'za'=4,'zb'=2,'y'=4,'core'=2] {'zb','y'}, dimensions={0} | all-to-all | bytes 2621440 | tf_op jit(solution)/shard_map/all_to_all | solution.py:23
  48.4 1.9 %collective-permute-start = (bf16[1024,640]{1,0:T(8,128)(2,1)S(1)}, bf16[1024,640]{1,0:T(8,128)(2,1)}, u32[]{:S(2)}, u32[]{:S(2)}) collective-permute-start(bf16[1024,640]{1,0:T(8,128)(2,1)S(1)} %bitcast.71), channel_id=1, source_target_pairs={{0,1},{1,0},{2,3},{3,2},{4,5},{5,4},{6,7},{7,6},{8,9},{9,8},{10,11... | collective-permute-start | bytes 3932168 | tf_op jit(solution)/shard_map/ppermute | solution.py:49
  50.4 0.0 copy-done.1
  50.4 0.1 constant_dynamic-slice_fusion
  50.6 0.5 fusion.12
  51.1 2.4 %collective-permute-done = bf16[1024,640]{1,0:T(8,128)(2,1)} collective-permute-done((bf16[1024,640]{1,0:T(8,128)(2,1)S(1)}, bf16[1024,640]{1,0:T(8,128)(2,1)}, u32[]{:S(2)}, u32[]{:S(2)}) %collective-permute-start) | collective-permute-done | bytes 1310752 | tf_op jit(solution)/shard_map/ppermute | solution.py:49
  53.5 1.9 %fusion = bf16[640,256]{1,0:T(8,128)(2,1)S(1)} fusion(f32[640,256]{1,0:T(8,128)S(1)} %fusion.12, bf16[1024,640]{1,0:T(8,128)(2,1)} %collective-permute-done, bf16[1024,256]{1,0:T(8,128)(2,1)S(1)} %bitcast.67), kind=kOutput, calls=%fused_computation.3 | convolution fusion | flops 335872000 | bytes 2818048 | tf_op jit(solution)/shard_map/dot_general | solution.py:52
  55.4 0.0 copy-start.2
  55.4 0.7 copy.28
  56.1 4.8 %all-to-all-start.2 = ((bf16[4,2,80,256]{3,2,1,0:T(8,128)(2,1)}), bf16[4,2,80,256]{3,2,1,0:T(8,128)(2,1)S(1)}, u32[]{:S(2)}, u32[]{:S(2)}) async-start(bf16[4,2,80,256]{3,2,1,0:T(8,128)(2,1)} %bitcast.61), calls=%async_computation.2 | async-start | bytes 655360 | tf_op jit(solution)/shard_map/all_to_all | solution.py:56
  60.9 0.0 copy-done.2
  60.9 5.6 %all-to-all-done.2 = bf16[4,2,80,256]{3,2,1,0:T(8,128)(2,1)S(1)} async-done(((bf16[4,2,80,256]{3,2,1,0:T(8,128)(2,1)}), bf16[4,2,80,256]{3,2,1,0:T(8,128)(2,1)S(1)}, u32[]{:S(2)}, u32[]{:S(2)}) %all-to-all-start.2) | async-done | bytes 327712 | tf_op jit(solution)/shard_map/all_to_all | solution.py:56
  66.6 9.8 %collective-permute-start.1 = (bf16[200,256]{1,0:T(8,128)(2,1)S(1)}, bf16[200,256]{1,0:T(8,128)(2,1)S(1)}, u32[]{:S(2)}, u32[]{:S(2)}) collective-permute-start(bf16[200,256]{1,0:T(8,128)(2,1)S(1)} %pad_maximum_fusion), channel_id=1, source_target_pairs={{0,64},{64,0},{1,65},{65,1},{2,66},{66,2},{3,67},{67,3},{4,68},{68... | collective-permute-start | bytes 307208 | tf_op jit(solution)/shard_map/ppermute | solution.py:57
  76.4 0.1 broadcast_in_dim.63
  76.4 0.1 broadcast_in_dim.64
  76.5 5.3 %collective-permute-done.1 = bf16[200,256]{1,0:T(8,128)(2,1)S(1)} collective-permute-done((bf16[200,256]{1,0:T(8,128)(2,1)S(1)}, bf16[200,256]{1,0:T(8,128)(2,1)S(1)}, u32[]{:S(2)}, u32[]{:S(2)}) %collective-permute-start.1) | collective-permute-done | bytes 102432 | tf_op jit(solution)/shard_map/ppermute | solution.py:57
  81.9 0.1 fusion.10
  82.1 8.5 %all_to_all.32 = bf16[4,80,256]{2,1,0:T(8,128)(2,1)S(1)} all-to-all(bf16[4,80,256]{2,1,0:T(8,128)(2,1)S(1)} %broadcast_in_dim.69), channel_id=1, replica_groups=mesh['x'=4,'zh'=2,'za'=4,'zb'=2,'y'=4,'core'=2] {'x'}, dimensions={0} | all-to-all | bytes 327680 | tf_op jit(solution)/shard_map/all_to_all | solution.py:23
  90.6 0.4 convolution_convert_fusion
  91.0 1.9 %collective-permute-start.2 = (bf16[1024,320]{0,1:T(8,128)(2,1)S(1)}, bf16[1024,320]{0,1:T(8,128)(2,1)S(1)}, u32[]{:S(2)}, u32[]{:S(2)}) collective-permute-start(bf16[1024,320]{0,1:T(8,128)(2,1)S(1)} %convolution_convert_fusion), channel_id=1, source_target_pairs={{0,1},{1,0},{2,3},{3,2},{4,5},{5,4},{6,7},{7,6},{8,9},{9,8},{10,11... | collective-permute-start | bytes 1966088 | tf_op jit(solution)/shard_map/ppermute | solution.py:73
  92.9 2.1 %collective-permute-done.2 = bf16[1024,320]{0,1:T(8,128)(2,1)S(1)} collective-permute-done((bf16[1024,320]{0,1:T(8,128)(2,1)S(1)}, bf16[1024,320]{0,1:T(8,128)(2,1)S(1)}, u32[]{:S(2)}, u32[]{:S(2)}) %collective-permute-start.2) | collective-permute-done | bytes 655392 | tf_op jit(solution)/shard_map/ppermute | solution.py:73
  95.0 0.4 fusion.1
  95.3 0.1 copy.27
  95.5 19.4 %all_to_all.33 = bf16[8,128,320]{1,2,0:T(8,128)(2,1)S(1)} all-to-all(bf16[8,128,320]{1,2,0:T(8,128)(2,1)S(1)} %bitcast.64), channel_id=1, replica_groups=mesh['x'=4,'zh'=2,'za'=4,'zb'=2,'y'=4,'core'=2] {'zb','y'}, dimensions={0} | all-to-all | bytes 1310720 | tf_op jit(solution)/shard_map/all_to_all | solution.py:75
  114.8 0.1 reduce_sum.34
  114.9 0.8 copy.20
  115.7 7.7 %all-to-all-start.5 = ((bf16[4,32,320]{2,1,0:T(8,128)(2,1)}), bf16[4,32,320]{2,1,0:T(8,128)(2,1)S(1)}, u32[]{:S(2)}, u32[]{:S(2)}) async-start(bf16[4,32,320]{2,1,0:T(8,128)(2,1)} %bitcast.23), calls=%async_computation.5 | async-start | bytes 196608 | tf_op jit(solution)/shard_map/all_to_all | solution.py:77
  123.4 0.6 dynamic-slice
  124.0 1.3 fusion.9
  125.3 8.7 %all-to-all-done.5 = bf16[4,32,320]{2,1,0:T(8,128)(2,1)S(1)} async-done(((bf16[4,32,320]{2,1,0:T(8,128)(2,1)}), bf16[4,32,320]{2,1,0:T(8,128)(2,1)S(1)}, u32[]{:S(2)}, u32[]{:S(2)}) %all-to-all-start.5) | async-done | bytes 81952 | tf_op jit(solution)/shard_map/all_to_all | solution.py:77
  134.0 0.8 convolution_bitcast_fusion
  (15 shorter events, 0.3 us)
Async XLA Ops:
  0.6 1.0 copy-start
  1.6 25.5 %copy-start.3 = (f32[320,32]{0,1:T(8,128)}, f32[320,32]{0,1:T(8,128)S(1)}, u32[]{:S(2)}) copy-start(f32[320,32]{0,1:T(8,128)S(1)} %multiply_add_fusion) | copy-start | bytes 122884
  27.2 23.2 %copy-start.1 = (bf16[2048,256]{1,0:T(8,128)(2,1)S(1)}, bf16[2048,256]{1,0:T(8,128)(2,1)}, u32[]{:S(2)}) copy-start(bf16[2048,256]{1,0:T(8,128)(2,1)} %param.9) | copy-start | bytes 3145732
  48.4 5.0 %collective-permute-start = (bf16[1024,640]{1,0:T(8,128)(2,1)S(1)}, bf16[1024,640]{1,0:T(8,128)(2,1)}, u32[]{:S(2)}, u32[]{:S(2)}) collective-permute-start(bf16[1024,640]{1,0:T(8,128)(2,1)S(1)} %bitcast.71), channel_id=1, source_target_pairs={{0,1},{1,0},{2,3},{3,2},{4,5},{5,4},{6,7},{7,6},{8,9},{9,8},{10,11... | collective-permute-start | bytes 3932168 | tf_op jit(solution)/shard_map/ppermute | solution.py:49
  55.4 5.5 %copy-start.2 = (f32[40,256]{1,0:T(8,128)S(1)}, f32[40,256]{1,0:T(8,128)}, u32[]{:S(2)}) copy-start(f32[40,256]{1,0:T(8,128)} %param.7) | copy-start | bytes 122884
  56.1 10.4 %all-to-all-start.2 = ((bf16[4,2,80,256]{3,2,1,0:T(8,128)(2,1)}), bf16[4,2,80,256]{3,2,1,0:T(8,128)(2,1)S(1)}, u32[]{:S(2)}, u32[]{:S(2)}) async-start(bf16[4,2,80,256]{3,2,1,0:T(8,128)(2,1)} %bitcast.61), calls=%async_computation.2 | async-start | bytes 655360 | tf_op jit(solution)/shard_map/all_to_all | solution.py:56
  66.6 15.3 %collective-permute-start.1 = (bf16[200,256]{1,0:T(8,128)(2,1)S(1)}, bf16[200,256]{1,0:T(8,128)(2,1)S(1)}, u32[]{:S(2)}, u32[]{:S(2)}) collective-permute-start(bf16[200,256]{1,0:T(8,128)(2,1)S(1)} %pad_maximum_fusion), channel_id=1, source_target_pairs={{0,64},{64,0},{1,65},{65,1},{2,66},{66,2},{3,67},{67,3},{4,68},{68... | collective-permute-start | bytes 307208 | tf_op jit(solution)/shard_map/ppermute | solution.py:57
  91.0 4.0 %collective-permute-start.2 = (bf16[1024,320]{0,1:T(8,128)(2,1)S(1)}, bf16[1024,320]{0,1:T(8,128)(2,1)S(1)}, u32[]{:S(2)}, u32[]{:S(2)}) collective-permute-start(bf16[1024,320]{0,1:T(8,128)(2,1)S(1)} %convolution_convert_fusion), channel_id=1, source_target_pairs={{0,1},{1,0},{2,3},{3,2},{4,5},{5,4},{6,7},{7,6},{8,9},{9,8},{10,11... | collective-permute-start | bytes 1966088 | tf_op jit(solution)/shard_map/ppermute | solution.py:73
  115.7 18.3 %all-to-all-start.5 = ((bf16[4,32,320]{2,1,0:T(8,128)(2,1)}), bf16[4,32,320]{2,1,0:T(8,128)(2,1)S(1)}, u32[]{:S(2)}, u32[]{:S(2)}) async-start(bf16[4,32,320]{2,1,0:T(8,128)(2,1)} %bitcast.23), calls=%async_computation.5 | async-start | bytes 196608 | tf_op jit(solution)/shard_map/all_to_all | solution.py:77

commit v3 on v2

v3 whole, which is shorter than its diff:
```python
import jax
import jax.numpy as jnp
from jax import lax
from jax.experimental import pallas as pl
from jax.experimental.pallas import tpu as pltpu
from jax.sharding import Mesh, PartitionSpec as P

beta_first = 0.95
beta_second = 0.95
epsilon_root = 1e-08

f32 = jnp.float32
bf16 = jnp.bfloat16
X, ZH, ZA, ZB, Y, C = 4, 2, 4, 2, 4, 2
SWAP = [(0, 1), (1, 0)]
VMEM = pl.BlockSpec(memory_space=pltpu.VMEM)
SMEM = pl.BlockSpec(memory_space=pltpu.SMEM)


def dot(left, right, over_left, over_right):
    return lax.dot_general(
        left, right, (((over_left,), (over_right,)), ((), ())), preferred_element_type=f32
    )


def local(body, outs, ins, scalars=0):
    shapes = tuple(jax.ShapeDtypeStruct(shape, dtype) for shape, dtype in outs)
    return pl.pallas_call(
        body,
        out_shape=shapes,
        in_specs=[SMEM] * scalars + [VMEM] * (len(ins) - scalars),
        out_specs=(VMEM,) * len(outs),
        compiler_params=pltpu.CompilerParams(vmem_limit_bytes=24 << 20),
    )(*ins)


def left_kernel(grad, moment, basis, momentum, sent):
    new = beta_first * moment[...] + (1.0 - beta_first) * grad[...].astype(f32)
    momentum[...] = new
    rotated_grad = dot(grad[...], basis[...], 1, 0).astype(bf16)
    rotated_moment = dot(new.astype(bf16), basis[...], 1, 0).astype(bf16)
    for i in range(ZA):
        sent[i, :, :320] = rotated_grad
        sent[i, :, 320:] = rotated_moment


def rows_of(basis, core):
    return jnp.concatenate(
        [basis[za * ZB * Y + k, core] for k in range(ZB * Y) for za in range(ZA)], axis=0
    )


def rotate_own_kernel(core, left, basis, part):
    part[...] = dot(left[...], rows_of(basis, core[0]), 0, 0)


def rotate_other_kernel(core, left, basis, part, sent):
    total = (part[...] + dot(left[...], rows_of(basis, 1 - core[0]), 0, 0)).astype(bf16)
    for x in range(X):
        sent[x, :80] = total[x * 80 : x * 80 + 80]
        sent[x, 80:] = total[320 + x * 80 : 400 + x * 80]


def sum_kernel(parts, second_moment, total, sent):
    value = jnp.sum(parts[...].astype(f32), axis=0)
    total[...] = value
    sent[...] = jnp.concatenate([value, second_moment[...]], axis=0).astype(bf16)


def direction_kernel(half, total, other, second_moment, second, sent):
    upper = half[0] == 0
    partner = other[...].astype(f32)
    summed = total[...] + partner[:160]
    mine, theirs = second_moment[...], partner[160:]
    before = jnp.where(
        upper, jnp.concatenate([mine, theirs], axis=0), jnp.concatenate([theirs, mine], axis=0)
    )
    after = beta_second * before + (1.0 - beta_second) * summed[:80] * summed[:80]
    second[...] = jnp.where(upper, after[:40], after[40:])
    direction = (summed[80:] / (jnp.sqrt(after) + epsilon_root)).astype(bf16)
    for i in range(X):
        sent[i] = direction


def back_other_kernel(core, direction, basis, sent):
    back = dot(direction[...], rows_of(basis, 1 - core[0]), 1, 1).astype(bf16)
    for k in range(ZB * Y):
        sent[k] = back[:, k * 128 : k * 128 + 128]


def back_own_kernel(core, direction, basis, received, sent):
    back = dot(direction[...], rows_of(basis, core[0]), 1, 1)
    for k in range(ZB * Y):
        sent[k] = (back[:, k * 128 : k * 128 + 128] + received[k].astype(f32)).astype(bf16)


def update_kernel(parts, basis, sent):
    back = jnp.sum(parts[...].astype(f32), axis=0).T.astype(bf16)
    update = dot(back, basis[...], 1, 1).astype(bf16)
    for i in range(ZA):
        sent[i] = update[i * 32 : i * 32 + 32]


def add_kernel(parts, total):
    total[...] = jnp.sum(parts[...].astype(f32), axis=0)


def spread(values, axis, count):
    return lax.all_to_all(
        jnp.broadcast_to(values[None], (count,) + values.shape), axis, 0, 0
    )


def per_device(grad, moment, second_moment, left_basis, right_basis):
    core = lax.axis_index("core").reshape(1)
    half = lax.axis_index("zh").reshape(1)
    basis = right_basis.reshape(ZA * ZB * Y, C, 32, 256)
    momentum, left = local(
        left_kernel,
        (((32, 320), f32), ((ZA, 32, 640), bf16)),
        (grad.T, moment.T, left_basis),
    )
    left = lax.all_to_all(left, "za", 0, 0).reshape(128, 640)
    left = spread(left, ("zb", "y"), ZB * Y).reshape(1024, 640)
    left_other = lax.ppermute(left, "core", SWAP)
    (part,) = local(rotate_own_kernel, (((640, 256), f32),), (core, left, basis), 1)
    (part,) = local(
        rotate_other_kernel, (((X, 160, 256), bf16),), (core, left_other, basis, part), 1
    )
    part = lax.all_to_all(part, "x", 0, 0)
    part, sent = local(
        sum_kernel, (((160, 256), f32), ((200, 256), bf16)), (part, second_moment)
    )
    other = lax.ppermute(sent, "zh", SWAP)
    second, direction = local(
        direction_kernel,
        (((40, 256), f32), ((X, 80, 256), bf16)),
        (half, part, other, second_moment),
        1,
    )
    direction = lax.all_to_all(direction, "x", 0, 0).reshape(320, 256)
    blocks = (((ZB * Y, 320, 128), bf16),)
    (sent,) = local(back_other_kernel, blocks, (core, direction, basis), 1)
    received = lax.ppermute(sent, "core", SWAP)
    (back,) = local(back_own_kernel, blocks, (core, direction, basis, received), 1)
    back = lax.all_to_all(back, ("zb", "y"), 0, 0)
    (update,) = local(update_kernel, (((ZA, 32, 320), bf16),), (back, left_basis))
    update = lax.all_to_all(update, "za", 0, 0)
    (update,) = local(add_kernel, (((32, 320), f32),), (update,))
    return (momentum.T, second, update.T)


def solution(mesh):
    names = ("x", "zh", "za", "zb", "y", "core")
    fine = Mesh(mesh.devices.reshape(X, ZH, ZA, ZB, Y, C), names)
    columns = P(None, names)
    block = P(("x", "zh"), ("za", "zb", "y", "core"))
    return jax.shard_map(
        per_device,
        mesh=fine,
        in_specs=(columns, columns, block, P(), block),
        out_specs=(columns, block, columns),
        check_vma=False,
    )
```

time: 136 us -> 135 us (level)
  blocking collectives: 73.4 us -> 101 us
  waiting for transfers between devices: 24 us -> 10.4 us
  starting transfers between devices: 26.1 us -> 13.7 us
  Pallas kernels: 0 us -> 5.45 us
  matrix products: 5 us -> 0 us
  other arithmetic: 2.56 us -> 0 us
    all_to_all x1 -> x5, blocking collectives: 19.4 us -> 79.8 us  [the longest x1 24.2 us: per_device(): left = lax.all_to_all(left, 'za', 0, 0).reshape(128, 640)]
    all_to_all x3 -> x1, blocking collectives: 54 us -> 21.3 us  [spread(): lax.all_to_all(jnp.broadcast_to(values[None], (count,) + values.shape), a...]
    all_to_all x2 -> x0, waiting for transfers between devices: 14.3 us -> none  [the longest x1 8.67 us: per_device(): back = add_up(lax.all_to_all(back, 'za', 0, 0)).astype(bf16)]
    all_to_all x2 -> x0, starting transfers between devices: 12.5 us -> none  [the longest x1 7.72 us: per_device(): back = add_up(lax.all_to_all(back, 'za', 0, 0)).astype(bf16)]
    pallas_call x0 -> x9, Pallas kernels: none -> 5.45 us  [local(): pl.pallas_call(body, out_shape=shapes, in_specs=[SMEM] * scalars + [VMEM]...]
    dot_general x7 -> x0, matrix products: 5 us -> none  [the longest x2 2.41 us: rotate(): lax.dot_general(piece, basis, (((0,), (0,)), ((), ())), preferred_element...]
    unnamed x10 -> x12, local copies, waits for them, and re-layouts: 0.2 us -> 2.49 us
  transfers between devices with their start and end apart: 5 -> 3, of which waited for: 5 -> 3; matrix products, arithmetic and copies ran while one was open for 2% -> 0% of each run, Pallas kernels for 0% -> 0%
where the time goes in v3:
time: 135 us; the launch traced here: 134 us
  blocking collectives  101 us (75%)
  starting transfers between devices  13.7 us (10%)
  waiting for transfers between devices  10.4 us (8%)
  Pallas kernels  5.45 us (4%)
  local copies, waits for them, and re-layouts  2.6 us (2%)
    all_to_all x1, blocking collectives, per_device(): left = lax.all_to_all(left, 'za', 0, 0).reshape(128, 640)  24.2 us
    all_to_all x1, blocking collectives, spread(): lax.all_to_all(jnp.broadcast_to(values[None], (count,) + values.shape), a...  21.3 us
    all_to_all x1, blocking collectives, per_device(): back = lax.all_to_all(back, ('zb', 'y'), 0, 0)  19.6 us
    all_to_all x1, blocking collectives, per_device(): update = lax.all_to_all(update, 'za', 0, 0)  17.2 us
    all_to_all x1, blocking collectives, per_device(): part = lax.all_to_all(part, 'x', 0, 0)  10.2 us
    ppermute x1, starting transfers between devices, per_device(): other = lax.ppermute(sent, 'zh', SWAP)  9.78 us
    all_to_all x1, blocking collectives, per_device(): direction = lax.all_to_all(direction, 'x', 0, 0).reshape(320, 256)  8.49 us
    ppermute x1, waiting for transfers between devices, per_device(): other = lax.ppermute(sent, 'zh', SWAP)  5.77 us
  transfers between devices with their start and end apart: 3, of which 3 were waited for; matrix products, arithmetic and copies ran while one was open for 0% of the time, Pallas kernels for 0%

profile of v3, /device:TPU:6, one launch (start us, length us, event | category | flops | bytes accessed | tf_op | source)
XLA Modules:
  0.0 134.0 jit_solution(18368004718682222714)
XLA Ops:
  0.6 0.0 copy-start.1
  0.6 0.9 copy-done.1
  1.6 0.0 copy-start.4
  1.6 0.8 copy-done.4
  2.4 0.0 copy-start.5
  2.4 0.7 copy-done.5
  3.1 0.7 shard_map.76
  3.8 24.2 %all_to_all.30 = bf16[4,32,640]{2,1,0:T(8,128)(2,1)S(1)} all-to-all(bf16[4,32,640]{2,1,0:T(8,128)(2,1)S(1)} %get-tuple-element.10), channel_id=1, replica_groups=mesh['x'=4,'zh'=2,'za'=4,'zb'=2,'y'=4,'core'=2] {'za'}, dimensions={0} | all-to-all | bytes 327680 | tf_op jit(solution)/shard_map/all_to_all | solution.py:123
  28.0 0.1 broadcast_in_dim.8
  28.1 0.0 copy-start
  28.1 21.3 %all_to_all.31 = bf16[8,128,640]{2,1,0:T(8,128)(2,1)S(1)} all-to-all(bf16[8,128,640]{2,1,0:T(8,128)(2,1)S(1)} %broadcast_in_dim.8), channel_id=1, replica_groups=mesh['x'=4,'zh'=2,'za'=4,'zb'=2,'y'=4,'core'=2] {'zb','y'}, dimensions={0} | all-to-all | bytes 2621440 | tf_op jit(solution)/shard_map/all_to_all | solution.py:109
  49.4 1.9 %collective-permute-start = (bf16[1024,640]{1,0:T(8,128)(2,1)S(1)}, bf16[1024,640]{1,0:T(8,128)(2,1)}, u32[]{:S(2)}, u32[]{:S(2)}) collective-permute-start(bf16[1024,640]{1,0:T(8,128)(2,1)S(1)} %bitcast.14), channel_id=1, source_target_pairs={{0,1},{1,0},{2,3},{3,2},{4,5},{5,4},{6,7},{7,6},{8,9},{9,8},{10,11... | collective-permute-start | bytes 3932168 | tf_op jit(solution)/shard_map/ppermute | solution.py:125
  51.3 0.0 copy-done
  51.3 0.5 shard_map.77.part
  51.9 0.0 copy-start.3
  51.9 2.5 %collective-permute-done.left = bf16[1024,640]{1,0:T(8,128)(2,1)} collective-permute-done((bf16[1024,640]{1,0:T(8,128)(2,1)S(1)}, bf16[1024,640]{1,0:T(8,128)(2,1)}, u32[]{:S(2)}, u32[]{:S(2)}) %collective-permute-start) | collective-permute-done | bytes 1310752 | tf_op jit(solution)/shard_map/ppermute | solution.py:125
  54.4 1.9 %shard_map.78 = bf16[4,160,256]{2,1,0:T(8,128)(2,1)S(1)} custom-call(s32[1]{0:T(128)} %bitcast.4.core, bf16[1024,640]{1,0:T(8,128)(2,1)} %collective-permute-done.left, bf16[32,2,32,256]{3,2,1,0:T(8,128)(2,1)S(1)} %bitcast.11, f32[640,256]{1,0:T(8,128)S(1)} %shard_map.77.part), custom_call_target="tpu_custom_call" | custom-call | tf_op jit(solution)/shard_map/pallas_call | solution.py:28
  56.3 10.2 %all_to_all.32.parts = bf16[4,160,256]{2,1,0:T(8,128)(2,1)S(1)} all-to-all(bf16[4,160,256]{2,1,0:T(8,128)(2,1)S(1)} %shard_map.78), channel_id=1, replica_groups=mesh['x'=4,'zh'=2,'za'=4,'zb'=2,'y'=4,'core'=2] {'x'}, dimensions={0} | all-to-all | bytes 655360 | tf_op jit(solution)/shard_map/all_to_all | solution.py:130
  66.5 0.0 copy-done.3
  66.5 9.8 %collective-permute-start.1 = (bf16[200,256]{1,0:T(8,128)(2,1)S(1)}, bf16[200,256]{1,0:T(8,128)(2,1)S(1)}, u32[]{:S(2)}, u32[]{:S(2)}) collective-permute-start(bf16[200,256]{1,0:T(8,128)(2,1)S(1)} %get-tuple-element.12), channel_id=1, source_target_pairs={{0,64},{64,0},{1,65},{65,1},{2,66},{66,2},{3,67},{67,3},{4,68},{68... | collective-permute-start | bytes 307208 | tf_op jit(solution)/shard_map/ppermute | solution.py:134
  76.3 5.8 %collective-permute-done.1.other = bf16[200,256]{1,0:T(8,128)(2,1)S(1)} collective-permute-done((bf16[200,256]{1,0:T(8,128)(2,1)S(1)}, bf16[200,256]{1,0:T(8,128)(2,1)S(1)}, u32[]{:S(2)}, u32[]{:S(2)}) %collective-permute-start.1) | collective-permute-done | bytes 102432 | tf_op jit(solution)/shard_map/ppermute | solution.py:134
  82.1 0.6 shard_map.80
  82.7 8.5 %all_to_all.33 = bf16[4,80,256]{2,1,0:T(8,128)(2,1)S(1)} all-to-all(bf16[4,80,256]{2,1,0:T(8,128)(2,1)S(1)} %get-tuple-element.14), channel_id=1, replica_groups=mesh['x'=4,'zh'=2,'za'=4,'zb'=2,'y'=4,'core'=2] {'x'}, dimensions={0} | all-to-all | bytes 327680 | tf_op jit(solution)/shard_map/all_to_all | solution.py:141
  91.2 0.4 shard_map.81
  91.6 0.0 copy-start.2
  91.6 2.1 %collective-permute-start.2 = (bf16[8,320,128]{2,1,0:T(8,128)(2,1)S(1)}, bf16[8,320,128]{2,1,0:T(8,128)(2,1)S(1)}, u32[]{:S(2)}, u32[]{:S(2)}) collective-permute-start(bf16[8,320,128]{2,1,0:T(8,128)(2,1)S(1)} %shard_map.81), channel_id=1, source_target_pairs={{0,1},{1,0},{2,3},{3,2},{4,5},{5,4},{6,7},{7,6},{8,9},{9,8},{10,11... | collective-permute-start | bytes 1966088 | tf_op jit(solution)/shard_map/ppermute | solution.py:144
  93.7 2.1 %collective-permute-done.2.received = bf16[8,320,128]{2,1,0:T(8,128)(2,1)S(1)} collective-permute-done((bf16[8,320,128]{2,1,0:T(8,128)(2,1)S(1)}, bf16[8,320,128]{2,1,0:T(8,128)(2,1)S(1)}, u32[]{:S(2)}, u32[]{:S(2)}) %collective-permute-start.2) | collective-permute-done | bytes 655392 | tf_op jit(solution)/shard_map/ppermute | solution.py:144
  95.8 0.4 shard_map.82
  96.1 19.6 %all_to_all.34.parts = bf16[8,320,128]{2,1,0:T(8,128)(2,1)S(1)} all-to-all(bf16[8,320,128]{2,1,0:T(8,128)(2,1)S(1)} %shard_map.82), channel_id=1, replica_groups=mesh['x'=4,'zh'=2,'za'=4,'zb'=2,'y'=4,'core'=2] {'zb','y'}, dimensions={0} | all-to-all | bytes 1310720 | tf_op jit(solution)/shard_map/all_to_all | solution.py:146
  115.8 0.0 copy-done.2
  115.8 0.3 shard_map.83
  116.1 17.2 %all_to_all.35.parts = bf16[4,32,320]{2,1,0:T(8,128)(2,1)S(1)} all-to-all(bf16[4,32,320]{2,1,0:T(8,128)(2,1)S(1)} %shard_map.83), channel_id=1, replica_groups=mesh['x'=4,'zh'=2,'za'=4,'zb'=2,'y'=4,'core'=2] {'za'}, dimensions={0} | all-to-all | bytes 163840 | tf_op jit(solution)/shard_map/all_to_all | solution.py:148
  133.3 0.6 shard_map.84
  (1 shorter events, 0.0 us)
Async XLA Ops:
  0.6 0.9 copy-start.1
  1.6 0.8 copy-start.4
  2.4 0.7 copy-start.5
  28.1 23.2 %copy-start = (bf16[2048,256]{1,0:T(8,128)(2,1)S(1)}, bf16[2048,256]{1,0:T(8,128)(2,1)}, u32[]{:S(2)}) copy-start(bf16[2048,256]{1,0:T(8,128)(2,1)} %param.9) | copy-start | bytes 3145732
  49.4 5.0 %collective-permute-start = (bf16[1024,640]{1,0:T(8,128)(2,1)S(1)}, bf16[1024,640]{1,0:T(8,128)(2,1)}, u32[]{:S(2)}, u32[]{:S(2)}) collective-permute-start(bf16[1024,640]{1,0:T(8,128)(2,1)S(1)} %bitcast.14), channel_id=1, source_target_pairs={{0,1},{1,0},{2,3},{3,2},{4,5},{5,4},{6,7},{7,6},{8,9},{9,8},{10,11... | collective-permute-start | bytes 3932168 | tf_op jit(solution)/shard_map/ppermute | solution.py:125
  51.9 14.6 %copy-start.3 = (f32[40,256]{1,0:T(8,128)S(1)}, f32[40,256]{1,0:T(8,128)}, u32[]{:S(2)}) copy-start(f32[40,256]{1,0:T(8,128)} %second_moment.3) | copy-start | bytes 122884
  66.5 15.6 %collective-permute-start.1 = (bf16[200,256]{1,0:T(8,128)(2,1)S(1)}, bf16[200,256]{1,0:T(8,128)(2,1)S(1)}, u32[]{:S(2)}, u32[]{:S(2)}) collective-permute-start(bf16[200,256]{1,0:T(8,128)(2,1)S(1)} %get-tuple-element.12), channel_id=1, source_target_pairs={{0,64},{64,0},{1,65},{65,1},{2,66},{66,2},{3,67},{67,3},{4,68},{68... | collective-permute-start | bytes 307208 | tf_op jit(solution)/shard_map/ppermute | solution.py:134
  91.6 24.2 %copy-start.2 = (bf16[320,320]{1,0:T(8,128)(2,1)S(1)}, bf16[320,320]{1,0:T(8,128)(2,1)}, u32[]{:S(2)}) copy-start(bf16[320,320]{1,0:T(8,128)(2,1)} %basis.3) | copy-start | bytes 614404
  91.6 4.1 %collective-permute-start.2 = (bf16[8,320,128]{2,1,0:T(8,128)(2,1)S(1)}, bf16[8,320,128]{2,1,0:T(8,128)(2,1)S(1)}, u32[]{:S(2)}, u32[]{:S(2)}) collective-permute-start(bf16[8,320,128]{2,1,0:T(8,128)(2,1)S(1)} %shard_map.81), channel_id=1, source_target_pairs={{0,1},{1,0},{2,3},{3,2},{4,5},{5,4},{6,7},{7,6},{8,9},{9,8},{10,11... | collective-permute-start | bytes 1966088 | tf_op jit(solution)/shard_map/ppermute | solution.py:144

commit v4 on v3

v4 whole, which is shorter than its diff:
```python
import jax
import jax.numpy as jnp
from jax import lax
from jax.experimental import pallas as pl
from jax.experimental.pallas import tpu as pltpu
from jax.sharding import Mesh, PartitionSpec as P

beta_first = 0.95
beta_second = 0.95
epsilon_root = 1e-08

f32 = jnp.float32
bf16 = jnp.bfloat16
X, ZH, ZA, ZB, Y, C = 4, 2, 4, 2, 4, 2
SWAP = [(0, 1), (1, 0)]
VMEM = pl.BlockSpec(memory_space=pltpu.VMEM)
HBM = pl.BlockSpec(memory_space=pltpu.HBM)
SMEM = pl.BlockSpec(memory_space=pltpu.SMEM)


def dot(left, right, over_left, over_right):
    return lax.dot_general(
        left, right, (((over_left,), (over_right,)), ((), ())), preferred_element_type=f32
    )


def local(body, outs, ins, scalars=0):
    shapes = tuple(jax.ShapeDtypeStruct(shape, dtype) for shape, dtype in outs)
    return pl.pallas_call(
        body,
        out_shape=shapes,
        in_specs=[SMEM] * scalars + [VMEM] * (len(ins) - scalars),
        out_specs=(VMEM,) * len(outs),
        compiler_params=pltpu.CompilerParams(vmem_limit_bytes=24 << 20),
    )(*ins)


def left_kernel(grad_hbm, moment_hbm, basis_hbm, momentum, sent, grad, moment, basis, sems):
    pairs = ((grad_hbm, grad), (basis_hbm, basis), (moment_hbm, moment))
    copies = [
        pltpu.make_async_copy(source, target, sems.at[i])
        for i, (source, target) in enumerate(pairs)
    ]
    for copy in copies:
        copy.start()
    for copy in copies:
        copy.wait()
    new = beta_first * moment[...] + (1.0 - beta_first) * grad[...].astype(f32)
    momentum[...] = new
    rotated_grad = dot(grad[...], basis[...], 1, 0).astype(bf16)
    rotated_moment = dot(new.astype(bf16), basis[...], 1, 0).astype(bf16)
    for i in range(ZA):
        sent[i, :, :320] = rotated_grad
        sent[i, :, 320:] = rotated_moment


def left_stage(grad, moment, basis):
    return pl.pallas_call(
        left_kernel,
        out_shape=(
            jax.ShapeDtypeStruct((32, 320), f32),
            jax.ShapeDtypeStruct((ZA, 32, 640), bf16),
        ),
        in_specs=[HBM] * 3,
        out_specs=(VMEM, VMEM),
        scratch_shapes=[
            pltpu.VMEM((32, 320), bf16),
            pltpu.VMEM((32, 320), f32),
            pltpu.VMEM((320, 320), bf16),
            pltpu.SemaphoreType.DMA((3,)),
        ],
        compiler_params=pltpu.CompilerParams(vmem_limit_bytes=56 << 20),
    )(grad, moment, basis)


def kept_rows(basis, pair, core):
    return jnp.concatenate(
        [basis[za, pair, y, core] for y in range(Y) for za in range(ZA)], axis=0
    )


def received_rows(received, core):
    return jnp.concatenate(
        [received[za, y, core] for y in range(Y) for za in range(ZA)], axis=0
    )


def rotate_own_kernel(place, left, basis, received, part):
    core, pair = place[0], place[1]
    part[0] = dot(left[...], kept_rows(basis, pair, core), 0, 0)
    part[1] = dot(left[...], received_rows(received, core), 0, 0)


def rotate_other_kernel(place, left, basis, received, part, sent):
    core, pair = place[0], place[1]
    kept = part[0] + dot(left[...], kept_rows(basis, pair, 1 - core), 0, 0)
    given = part[1] + dot(left[...], received_rows(received, 1 - core), 0, 0)
    for to, total in ((pair, kept.astype(bf16)), (1 - pair, given.astype(bf16))):
        for x in range(X):
            sent[x * ZB + to, :80] = total[x * 80 : x * 80 + 80]
            sent[x * ZB + to, 80:] = total[320 + x * 80 : 400 + x * 80]


def sum_kernel(parts, second_moment, total, sent):
    value = jnp.sum(parts[...].astype(f32), axis=0)
    total[...] = value
    sent[...] = jnp.concatenate([value, second_moment[...]], axis=0).astype(bf16)


def direction_kernel(half, total, both, second_moment, second, sent):
    upper = half[0] == 0
    partner = both[1 - half[0]].astype(f32)
    summed = total[...] + partner[:160]
    mine, theirs = second_moment[...], partner[160:]
    before = jnp.where(
        upper, jnp.concatenate([mine, theirs], axis=0), jnp.concatenate([theirs, mine], axis=0)
    )
    after = beta_second * before + (1.0 - beta_second) * summed[:80] * summed[:80]
    second[...] = jnp.where(upper, after[:40], after[40:])
    direction = (summed[80:] / (jnp.sqrt(after) + epsilon_root)).astype(bf16)
    for i in range(X * ZB):
        sent[i] = direction


def back_rotate(pair, core, direction, basis, received):
    def columns(which):
        return jnp.concatenate([direction[x * ZB + which] for x in range(X)], axis=0)

    back = dot(columns(pair), kept_rows(basis, pair, core), 1, 1)
    return back + dot(columns(1 - pair), received_rows(received, core), 1, 1)


def back_other_kernel(place, direction, basis, received, sent):
    back = back_rotate(place[1], 1 - place[0], direction, basis, received).astype(bf16)
    for y in range(Y):
        sent[y] = back[:, y * 128 : y * 128 + 128]


def back_own_kernel(place, direction, basis, received, other, sent):
    back = back_rotate(place[1], place[0], direction, basis, received)
    for y in range(Y):
        sent[y] = (back[:, y * 128 : y * 128 + 128] + other[y].astype(f32)).astype(bf16)


def update_kernel(parts, basis, sent):
    back = jnp.sum(parts[...].astype(f32), axis=0).T.astype(bf16)
    update = dot(back, basis[...], 1, 1).astype(bf16)
    for i in range(ZA):
        sent[i] = update[i * 32 : i * 32 + 32]


def add_kernel(parts, total):
    total[...] = jnp.sum(parts[...].astype(f32), axis=0)


def spread(values, axis, count):
    return lax.all_to_all(
        jnp.broadcast_to(values[None], (count,) + values.shape), axis, 0, 0
    )


def per_device(grad, moment, second_moment, left_basis, right_basis):
    pair = lax.axis_index("zb")
    place = jnp.stack([lax.axis_index("core"), pair])
    half = lax.axis_index("zh").reshape(1)
    momentum, left = left_stage(grad.T, moment.T, left_basis)
    left = lax.all_to_all(left, "za", 0, 0).reshape(128, 640)
    basis = right_basis.reshape(ZA, ZB, Y, C, 32, 256)
    leaving = lax.dynamic_index_in_dim(basis, 1 - pair, 1, keepdims=False)
    received = lax.ppermute(leaving, "zb", SWAP)
    left = spread(left, "y", Y).reshape(512, 640)
    left, received = lax.optimization_barrier((left, received))
    left_other = lax.ppermute(left, "core", SWAP)
    (part,) = local(
        rotate_own_kernel, (((ZB, 640, 256), f32),), (place, left, basis, received), 1
    )
    (part,) = local(
        rotate_other_kernel,
        (((X * ZB, 160, 256), bf16),),
        (place, left_other, basis, received, part),
        1,
    )
    part = lax.all_to_all(part, ("x", "zb"), 0, 0)
    part, sent = local(
        sum_kernel, (((160, 256), f32), ((200, 256), bf16)), (part, second_moment)
    )
    both = lax.all_gather(sent, "zh")
    second, direction = local(
        direction_kernel,
        (((40, 256), f32), ((X * ZB, 80, 256), bf16)),
        (half, part, both, second_moment),
        1,
    )
    direction = lax.all_to_all(direction, ("x", "zb"), 0, 0)
    blocks = (((Y, 320, 128), bf16),)
    operands = (place, direction, basis, received)
    (sent,) = local(back_other_kernel, blocks, operands, 1)
    other = lax.ppermute(sent, "core", SWAP)
    (back,) = local(back_own_kernel, blocks, (*operands, other), 1)
    back = lax.all_to_all(back, "y", 0, 0)
    (update,) = local(update_kernel, (((ZA, 32, 320), bf16),), (back, left_basis))
    update = lax.all_to_all(update, "za", 0, 0)
    (update,) = local(add_kernel, (((32, 320), f32),), (update,))
    return (momentum.T, second, update.T)


def solution(mesh):
    names = ("x", "zh", "za", "zb", "y", "core")
    fine = Mesh(mesh.devices.reshape(X, ZH, ZA, ZB, Y, C), names)
    columns = P(None, names)
    block = P(("x", "zh"), ("za", "zb", "y", "core"))
    return jax.shard_map(
        per_device,
        mesh=fine,
        in_specs=(columns, columns, block, P(), block),
        out_specs=(columns, block, columns),
        check_vma=False,
    )
```

time: 135 us -> 127 us (0.941)
  blocking collectives: 101 us -> 56.2 us
  waiting for transfers between devices: 10.4 us -> 28.5 us
  starting transfers between devices: 13.7 us -> 29.9 us
  Pallas kernels: 5.45 us -> 8.45 us
    all_to_all x5 -> x2, blocking collectives: 83.8 us -> 23.7 us  [the longest x1 13.3 us: per_device(): direction = lax.all_to_all(direction, ('x', 'zb'), 0, 0)]
    all_to_all x0 -> x3, waiting for transfers between devices: none -> 25.9 us  [the longest x1 9.41 us: per_device(): part = lax.all_to_all(part, ('x', 'zb'), 0, 0)]
    all_to_all x0 -> x3, starting transfers between devices: none -> 22 us  [the longest x1 11.2 us: per_device(): left = lax.all_to_all(left, 'za', 0, 0).reshape(128, 640)]
    all_gather x0 -> x1, blocking collectives: none -> 17.5 us  [per_device(): both = lax.all_gather(sent, 'zh')]
    ppermute x2, waiting for transfers between devices: 7.84 us -> 1.77 us  [the longest x1 1.59 us: per_device(): other = lax.ppermute(sent, 'core', SWAP)]
    ppermute x2, starting transfers between devices: 11.8 us -> 6.01 us  [the longest x1 3.96 us: per_device(): received = lax.ppermute(leaving, 'zb', SWAP)]
    unnamed x12 -> x6, local copies, waits for them, and re-layouts: 2.49 us -> 0.02 us
    all_to_all x1, blocking collectives: 17.2 us -> 15.1 us  [per_device(): update = lax.all_to_all(update, 'za', 0, 0)]
  transfers between devices with their start and end apart: 3 -> 6, of which waited for: 3 -> 6; matrix products, arithmetic and copies ran while one was open for 0% -> 2% of each run, Pallas kernels for 0% -> 1%
where the time goes in v4:
time: 127 us; the launch traced here: 126 us
  blocking collectives  56.2 us (44%)
  starting transfers between devices  29.9 us (24%)
  waiting for transfers between devices  28.5 us (22%)
  Pallas kernels  8.45 us (7%)
  local copies, waits for them, and re-layouts  1.99 us (2%)
    all_gather x1, blocking collectives, per_device(): both = lax.all_gather(sent, 'zh')  17.5 us
    all_to_all x1, blocking collectives, per_device(): update = lax.all_to_all(update, 'za', 0, 0)  15.1 us
    all_to_all x1, blocking collectives, per_device(): direction = lax.all_to_all(direction, ('x', 'zb'), 0, 0)  13.3 us
    all_to_all x1, starting transfers between devices, per_device(): left = lax.all_to_all(left, 'za', 0, 0).reshape(128, 640)  11.2 us
    all_to_all x1, blocking collectives, per_device(): back = lax.all_to_all(back, 'y', 0, 0)  10.3 us
    all_to_all x1, waiting for transfers between devices, per_device(): part = lax.all_to_all(part, ('x', 'zb'), 0, 0)  9.41 us
    all_to_all x1, waiting for transfers between devices, spread(): lax.all_to_all(jnp.broadcast_to(values[None], (count,) + values.shape), a...  8.61 us
    all_to_all x1, waiting for transfers between devices, per_device(): left = lax.all_to_all(left, 'za', 0, 0).reshape(128, 640)  7.87 us
  transfers between devices with their start and end apart: 6, of which 6 were waited for; matrix products, arithmetic and copies ran while one was open for 2% of the time, Pallas kernels for 1%

profile of v4, /device:TPU:6, one launch (start us, length us, event | category | flops | bytes accessed | tf_op | source)
XLA Modules:
  0.0 125.9 jit_solution(8482177158382402220)
XLA Ops:
  0.6 1.9 %shard_map.76 = (f32[32,320]{1,0:T(8,128)}, bf16[4,32,640]{2,1,0:T(8,128)(2,1)}) custom-call(bf16[32,320]{1,0:T(8,128)(2,1)} %bitcast.24, f32[32,320]{1,0:T(8,128)} %bitcast.22, bf16[320,320]{1,0:T(8,128)(2,1)} %basis.1), custom_call_target="tpu_custom_call" | custom-call | tf_op jit(solution)/shard_map/pallas_call | solution.py:58
  2.6 11.2 %all-to-all-start = ((bf16[4,32,640]{2,1,0:T(8,128)(2,1)}), bf16[4,32,640]{2,1,0:T(8,128)(2,1)S(1)}, u32[]{:S(2)}, u32[]{:S(2)}) async-start(bf16[4,32,640]{2,1,0:T(8,128)(2,1)} %get-tuple-element.12), calls=%async_computation | async-start | bytes 327680 | tf_op jit(solution)/shard_map/all_to_all | solution.py:167
  13.7 1.1 dynamic-slice_bitcast_fusion
  14.8 0.0 copy-start
  14.8 4.0 %collective-permute-start = (bf16[4,4,2,32,256]{4,3,2,1,0:T(8,128)(2,1)S(1)}, bf16[4,4,2,32,256]{4,3,2,1,0:T(8,128)(2,1)S(1)}, u32[]{:S(2)}, u32[]{:S(2)}) collective-permute-start(bf16[4,4,2,32,256]{4,3,2,1,0:T(8,128)(2,1)S(1)} %dynamic-slice_bitcast_fusion), channel_id=1, source_target_pairs={{0,8},{8,0},{1,9},{9,1},{2,10},{10,2},{3,11},{11,3},{4,12},{12,4},... | collective-permute-start | bytes 1572872 | tf_op jit(solution)/shard_map/ppermute | solution.py:170
  18.8 7.9 %all-to-all-done = bf16[4,32,640]{2,1,0:T(8,128)(2,1)S(1)} async-done(((bf16[4,32,640]{2,1,0:T(8,128)(2,1)}), bf16[4,32,640]{2,1,0:T(8,128)(2,1)S(1)}, u32[]{:S(2)}, u32[]{:S(2)}) %all-to-all-start) | async-done | bytes 163872 | tf_op jit(solution)/shard_map/all_to_all | solution.py:167
  26.7 0.9 broadcast_in_dim.8
  27.6 4.5 %all-to-all-start.1 = ((bf16[4,128,640]{2,1,0:T(8,128)(2,1)}), bf16[4,128,640]{2,1,0:T(8,128)(2,1)S(1)}, u32[]{:S(2)}, u32[]{:S(2)}) async-start(bf16[4,128,640]{2,1,0:T(8,128)(2,1)} %broadcast_in_dim.8), calls=%async_computation.1 | async-start | bytes 1310720 | tf_op jit(solution)/shard_map/all_to_all | solution.py:157
  32.0 0.2 collective-permute-done.received
  32.2 8.6 %all-to-all-done.1 = bf16[4,128,640]{2,1,0:T(8,128)(2,1)S(1)} async-done(((bf16[4,128,640]{2,1,0:T(8,128)(2,1)}), bf16[4,128,640]{2,1,0:T(8,128)(2,1)S(1)}, u32[]{:S(2)}, u32[]{:S(2)}) %all-to-all-start.1) | async-done | bytes 655392 | tf_op jit(solution)/shard_map/all_to_all | solution.py:157
  40.8 1.9 %collective-permute-start.1 = (bf16[512,640]{1,0:T(8,128)(2,1)S(1)}, bf16[512,640]{1,0:T(8,128)(2,1)S(1)}, u32[]{:S(2)}, u32[]{:S(2)}) collective-permute-start(bf16[512,640]{1,0:T(8,128)(2,1)S(1)} %bitcast.18), channel_id=1, source_target_pairs={{0,1},{1,0},{2,3},{3,2},{4,5},{5,4},{6,7},{7,6},{8,9},{9,8},{10,11... | collective-permute-start | bytes 1966088 | tf_op jit(solution)/shard_map/ppermute | solution.py:173
  42.7 0.1 pad_add_fusion.place
  42.8 0.0 copy-done
  42.8 1.1 shard_map.77.part
  43.9 0.9 collective-permute-done.1.left
  44.8 2.0 %shard_map.78 = bf16[8,160,256]{2,1,0:T(8,128)(2,1)} custom-call(s32[2]{0:T(128)S(1)} %pad_add_fusion.place, bf16[512,640]{1,0:T(8,128)(2,1)S(1)} %collective-permute-done.1.left, bf16[4,2,4,2,32,256]{5,4,3,2,1,0:T(8,128)(2,1)S(1)} %bitcast.15, bf16[4,4,2,32,256]{4,3,2,1,0:T(8,128)(2,1)S(1)} %collective-permute-done.received, f32[2,640,256]{2,1,0:T(8,128)S(1)} %shard_map.77.part), custom_call_target="tpu_custom_call" | custom-call | tf_op jit(solution)/shard_map/pallas_call | solution.py:29
  46.8 0.0 copy-start.2
  46.8 6.3 %all-to-all-start.2 = ((bf16[8,160,256]{2,1,0:T(8,128)(2,1)}), bf16[8,160,256]{2,1,0:T(8,128)(2,1)S(1)}, u32[]{:S(2)}, u32[]{:S(2)}) async-start(bf16[8,160,256]{2,1,0:T(8,128)(2,1)} %shard_map.78), calls=%async_computation.2 | async-start | bytes 1310720 | tf_op jit(solution)/shard_map/all_to_all | solution.py:183
  53.1 9.4 %all-to-all-done.2.parts = bf16[8,160,256]{2,1,0:T(8,128)(2,1)S(1)} async-done(((bf16[8,160,256]{2,1,0:T(8,128)(2,1)}), bf16[8,160,256]{2,1,0:T(8,128)(2,1)S(1)}, u32[]{:S(2)}, u32[]{:S(2)}) %all-to-all-start.2) | async-done | bytes 655392 | tf_op jit(solution)/shard_map/all_to_all | solution.py:183
  62.5 0.0 copy-done.2
  62.5 0.1 shard_map.79
  62.6 17.5 %all-gather = bf16[400,256]{1,0:T(8,128)(2,1)S(1)} all-gather(bf16[200,256]{1,0:T(8,128)(2,1)S(1)} %get-tuple-element.16), channel_id=2, replica_groups=mesh['x'=4,'zh'=2,'za'=4,'zb'=2,'y'=4,'core'=2] {'zh'}, dimensions={0}, use_global_device_ids=true | all-gather | bytes 307200 | tf_op jit(solution)/shard_map/all_gather | solution.py:187
  80.1 0.7 shard_map.80
  80.7 13.3 %all_to_all.30.direction = bf16[8,80,256]{2,1,0:T(8,128)(2,1)S(1)} all-to-all(bf16[8,80,256]{2,1,0:T(8,128)(2,1)S(1)} %get-tuple-element.18), channel_id=1, replica_groups=mesh['x'=4,'zh'=2,'za'=4,'zb'=2,'y'=4,'core'=2] {'x','zb'}, dimensions={0} | all-to-all | bytes 655360 | tf_op jit(solution)/shard_map/all_to_all | solution.py:194
  94.1 0.9 shard_map.81
  95.0 0.0 copy-start.1
  95.0 2.1 %collective-permute-start.2 = (bf16[4,320,128]{2,1,0:T(8,128)(2,1)S(1)}, bf16[4,320,128]{2,1,0:T(8,128)(2,1)S(1)}, u32[]{:S(2)}, u32[]{:S(2)}) collective-permute-start(bf16[4,320,128]{2,1,0:T(8,128)(2,1)S(1)} %shard_map.81), channel_id=1, source_target_pairs={{0,1},{1,0},{2,3},{3,2},{4,5},{5,4},{6,7},{7,6},{8,9},{9,8},{10,11... | collective-permute-start | bytes 983048 | tf_op jit(solution)/shard_map/ppermute | solution.py:198
  97.1 1.6 %collective-permute-done.2.other = bf16[4,320,128]{2,1,0:T(8,128)(2,1)S(1)} collective-permute-done((bf16[4,320,128]{2,1,0:T(8,128)(2,1)S(1)}, bf16[4,320,128]{2,1,0:T(8,128)(2,1)S(1)}, u32[]{:S(2)}, u32[]{:S(2)}) %collective-permute-start.2) | collective-permute-done | bytes 327712 | tf_op jit(solution)/shard_map/ppermute | solution.py:198
  98.7 0.9 shard_map.82
  99.6 10.3 %all_to_all.31.parts = bf16[4,320,128]{2,1,0:T(8,128)(2,1)S(1)} all-to-all(bf16[4,320,128]{2,1,0:T(8,128)(2,1)S(1)} %shard_map.82), channel_id=1, replica_groups=mesh['x'=4,'zh'=2,'za'=4,'zb'=2,'y'=4,'core'=2] {'y'}, dimensions={0} | all-to-all | bytes 655360 | tf_op jit(solution)/shard_map/all_to_all | solution.py:200
  109.9 0.0 copy-done.1
  109.9 0.3 shard_map.83
  110.2 15.1 %all_to_all.32.parts = bf16[4,32,320]{2,1,0:T(8,128)(2,1)S(1)} all-to-all(bf16[4,32,320]{2,1,0:T(8,128)(2,1)S(1)} %shard_map.83), channel_id=1, replica_groups=mesh['x'=4,'zh'=2,'za'=4,'zb'=2,'y'=4,'core'=2] {'za'}, dimensions={0} | all-to-all | bytes 163840 | tf_op jit(solution)/shard_map/all_to_all | solution.py:202
  125.3 0.6 shard_map.84
Async XLA Ops:
  2.6 24.1 %all-to-all-start = ((bf16[4,32,640]{2,1,0:T(8,128)(2,1)}), bf16[4,32,640]{2,1,0:T(8,128)(2,1)S(1)}, u32[]{:S(2)}, u32[]{:S(2)}) async-start(bf16[4,32,640]{2,1,0:T(8,128)(2,1)} %get-tuple-element.12), calls=%async_computation | async-start | bytes 327680 | tf_op jit(solution)/shard_map/all_to_all | solution.py:167
  14.8 28.0 %copy-start = (bf16[2048,256]{1,0:T(8,128)(2,1)S(1)}, bf16[2048,256]{1,0:T(8,128)(2,1)}, u32[]{:S(2)}) copy-start(bf16[2048,256]{1,0:T(8,128)(2,1)} %param.9) | copy-start | bytes 3145732
  14.8 17.4 %collective-permute-start = (bf16[4,4,2,32,256]{4,3,2,1,0:T(8,128)(2,1)S(1)}, bf16[4,4,2,32,256]{4,3,2,1,0:T(8,128)(2,1)S(1)}, u32[]{:S(2)}, u32[]{:S(2)}) collective-permute-start(bf16[4,4,2,32,256]{4,3,2,1,0:T(8,128)(2,1)S(1)} %dynamic-slice_bitcast_fusion), channel_id=1, source_target_pairs={{0,8},{8,0},{1,9},{9,1},{2,10},{10,2},{3,11},{11,3},{4,12},{12,4},... | collective-permute-start | bytes 1572872 | tf_op jit(solution)/shard_map/ppermute | solution.py:170
  27.6 13.2 %all-to-all-start.1 = ((bf16[4,128,640]{2,1,0:T(8,128)(2,1)}), bf16[4,128,640]{2,1,0:T(8,128)(2,1)S(1)}, u32[]{:S(2)}, u32[]{:S(2)}) async-start(bf16[4,128,640]{2,1,0:T(8,128)(2,1)} %broadcast_in_dim.8), calls=%async_computation.1 | async-start | bytes 1310720 | tf_op jit(solution)/shard_map/all_to_all | solution.py:157
  40.8 4.0 %collective-permute-start.1 = (bf16[512,640]{1,0:T(8,128)(2,1)S(1)}, bf16[512,640]{1,0:T(8,128)(2,1)S(1)}, u32[]{:S(2)}, u32[]{:S(2)}) collective-permute-start(bf16[512,640]{1,0:T(8,128)(2,1)S(1)} %bitcast.18), channel_id=1, source_target_pairs={{0,1},{1,0},{2,3},{3,2},{4,5},{5,4},{6,7},{7,6},{8,9},{9,8},{10,11... | collective-permute-start | bytes 1966088 | tf_op jit(solution)/shard_map/ppermute | solution.py:173
  46.8 15.7 %copy-start.2 = (f32[40,256]{1,0:T(8,128)S(1)}, f32[40,256]{1,0:T(8,128)}, u32[]{:S(2)}) copy-start(f32[40,256]{1,0:T(8,128)} %second_moment.3) | copy-start | bytes 122884
  46.8 15.7 %all-to-all-start.2 = ((bf16[8,160,256]{2,1,0:T(8,128)(2,1)}), bf16[8,160,256]{2,1,0:T(8,128)(2,1)S(1)}, u32[]{:S(2)}, u32[]{:S(2)}) async-start(bf16[8,160,256]{2,1,0:T(8,128)(2,1)} %shard_map.78), calls=%async_computation.2 | async-start | bytes 1310720 | tf_op jit(solution)/shard_map/all_to_all | solution.py:183
  95.0 14.9 %copy-start.1 = (bf16[320,320]{1,0:T(8,128)(2,1)S(1)}, bf16[320,320]{1,0:T(8,128)(2,1)}, u32[]{:S(2)}) copy-start(bf16[320,320]{1,0:T(8,128)(2,1)} %basis.1) | copy-start | bytes 614404
  95.0 3.7 %collective-permute-start.2 = (bf16[4,320,128]{2,1,0:T(8,128)(2,1)S(1)}, bf16[4,320,128]{2,1,0:T(8,128)(2,1)S(1)}, u32[]{:S(2)}, u32[]{:S(2)}) collective-permute-start(bf16[4,320,128]{2,1,0:T(8,128)(2,1)S(1)} %shard_map.81), channel_id=1, source_target_pairs={{0,1},{1,0},{2,3},{3,2},{4,5},{5,4},{6,7},{7,6},{8,9},{9,8},{10,11... | collective-permute-start | bytes 983048 | tf_op jit(solution)/shard_map/ppermute | solution.py:198

commit v5 on v4

--- a/solution.py
+++ b/solution.py
@@ -107,9 +107,9 @@
     sent[...] = jnp.concatenate([value, second_moment[...]], axis=0).astype(bf16)
 
 
-def direction_kernel(half, total, both, second_moment, second, sent):
-    upper = half[0] == 0
-    partner = both[1 - half[0]].astype(f32)
+def direction_kernel(place, total, both, second_moment, second, sent):
+    upper = place[2] == 0
+    partner = both[1 - place[2]].astype(f32)
     summed = total[...] + partner[:160]
     mine, theirs = second_moment[...], partner[160:]
     before = jnp.where(
@@ -136,21 +136,33 @@
         sent[y] = back[:, y * 128 : y * 128 + 128]
 
 
-def back_own_kernel(place, direction, basis, received, other, sent):
+def back_own_kernel(place, direction, basis, received, part):
     back = back_rotate(place[1], place[0], direction, basis, received)
     for y in range(Y):
-        sent[y] = (back[:, y * 128 : y * 128 + 128] + other[y].astype(f32)).astype(bf16)
+        part[y] = back[:, y * 128 : y * 128 + 128]
+
+
+def back_add_kernel(part, other, sent):
+    sent[...] = (part[...] + other[...].astype(f32)).astype(bf16)
 
 
 def update_kernel(parts, basis, sent):
     back = jnp.sum(parts[...].astype(f32), axis=0).T.astype(bf16)
     update = dot(back, basis[...], 1, 1).astype(bf16)
     for i in range(ZA):
-        sent[i] = update[i * 32 : i * 32 + 32]
+        block = update[i * 32 : i * 32 + 32]
+        to = ZA - 1 - i
+        sent[to, :32] = block[:, :128]
+        sent[to, 32:64] = block[:, 128:256]
+        sent[to, 64:] = jnp.concatenate([block[:16, 256:], block[16:, 256:]], axis=1)
 
 
 def add_kernel(parts, total):
-    total[...] = jnp.sum(parts[...].astype(f32), axis=0)
+    value = jnp.sum(parts[...].astype(f32), axis=0)
+    total[:, :128] = value[:32]
+    total[:, 128:256] = value[32:64]
+    total[:16, 256:] = value[64:, :64]
+    total[16:, 256:] = value[64:, 64:]
 
 
 def spread(values, axis, count):
@@ -161,8 +173,7 @@
 
 def per_device(grad, moment, second_moment, left_basis, right_basis):
     pair = lax.axis_index("zb")
-    place = jnp.stack([lax.axis_index("core"), pair])
-    half = lax.axis_index("zh").reshape(1)
+    place = jnp.stack([lax.axis_index("core"), pair, lax.axis_index("zh")])
     momentum, left = left_stage(grad.T, moment.T, left_basis)
     left = lax.all_to_all(left, "za", 0, 0).reshape(128, 640)
     basis = right_basis.reshape(ZA, ZB, Y, C, 32, 256)
@@ -188,7 +199,7 @@
     second, direction = local(
         direction_kernel,
         (((40, 256), f32), ((X * ZB, 80, 256), bf16)),
-        (half, part, both, second_moment),
+        (place, part, both, second_moment),
         1,
     )
     direction = lax.all_to_all(direction, ("x", "zb"), 0, 0)
@@ -196,10 +207,11 @@
     operands = (place, direction, basis, received)
     (sent,) = local(back_other_kernel, blocks, operands, 1)
     other = lax.ppermute(sent, "core", SWAP)
-    (back,) = local(back_own_kernel, blocks, (*operands, other), 1)
+    (part,) = local(back_own_kernel, (((Y, 320, 128), f32),), operands, 1)
+    (back,) = local(back_add_kernel, blocks, (part, other))
     back = lax.all_to_all(back, "y", 0, 0)
-    (update,) = local(update_kernel, (((ZA, 32, 320), bf16),), (back, left_basis))
-    update = lax.all_to_all(update, "za", 0, 0)
+    (update,) = local(update_kernel, (((ZA, 80, 128), bf16),), (back, left_basis))
+    update = lax.all_to_all(update, "za", 0, 0, axis_index_groups=[[3, 2, 1, 0]])
     (update,) = local(add_kernel, (((32, 320), f32),), (update,))
     return (momentum.T, second, update.T)
 

time: 127 us -> 122 us (0.961)
  blocking collectives: 56.2 us -> 68.2 us
  waiting for transfers between devices: 28.5 us -> 18.2 us
  starting transfers between devices: 29.9 us -> 23.4 us
    all_to_all x1 -> x2, blocking collectives: 15.1 us -> 28.4 us  [the longest x1 15.7 us: per_device(): part = lax.all_to_all(part, ('x', 'zb'), 0, 0)]
    all_to_all x1 -> x0, waiting for transfers between devices: 9.41 us -> none  [per_device(): part = lax.all_to_all(part, ('x', 'zb'), 0, 0)]
    all_to_all x1 -> x0, starting transfers between devices: 6.33 us -> none  [per_device(): part = lax.all_to_all(part, ('x', 'zb'), 0, 0)]
    pallas_call x8 -> x9, Pallas kernels: 6.54 us -> 6.4 us  [local(): pl.pallas_call(body, out_shape=shapes, in_specs=[SMEM] * scalars + [VMEM]...]
  transfers between devices with their start and end apart: 6 -> 5, of which waited for: 6 -> 5; matrix products, arithmetic and copies ran while one was open for 2% -> 2% of each run, Pallas kernels for 1% -> 2%
where the time goes in v5:
time: 122 us; the launch traced here: 121 us
  blocking collectives  68.2 us (56%)
  starting transfers between devices  23.4 us (19%)
  waiting for transfers between devices  18.2 us (15%)
  Pallas kernels  8.32 us (7%)
  local copies, waits for them, and re-layouts  1.99 us (2%)
    all_gather x1, blocking collectives, per_device(): both = lax.all_gather(sent, 'zh')  17.2 us
    all_to_all x1, blocking collectives, per_device(): part = lax.all_to_all(part, ('x', 'zb'), 0, 0)  15.7 us
    all_to_all x1, blocking collectives, per_device(): lax.all_to_all(update, 'za', 0, 0, axis_index_groups=[[3, 2, 1, 0]])  12.7 us
    all_to_all x1, blocking collectives, per_device(): direction = lax.all_to_all(direction, ('x', 'zb'), 0, 0)  12.3 us
    all_to_all x1, starting transfers between devices, per_device(): left = lax.all_to_all(left, 'za', 0, 0).reshape(128, 640)  11.2 us
    all_to_all x1, blocking collectives, per_device(): back = lax.all_to_all(back, 'y', 0, 0)  10.3 us
    all_to_all x1, waiting for transfers between devices, spread(): lax.all_to_all(jnp.broadcast_to(values[None], (count,) + values.shape), a...  8.6 us
    all_to_all x1, waiting for transfers between devices, per_device(): left = lax.all_to_all(left, 'za', 0, 0).reshape(128, 640)  7.87 us
  transfers between devices with their start and end apart: 5, of which 5 were waited for; matrix products, arithmetic and copies ran while one was open for 2% of the time, Pallas kernels for 2%

profile of v5, /device:TPU:6, one launch (start us, length us, event | category | flops | bytes accessed | tf_op | source)
XLA Modules:
  0.0 121.0 jit_solution(8315490207911302696)
XLA Ops:
  0.6 1.9 %shard_map.76 = (f32[32,320]{1,0:T(8,128)}, bf16[4,32,640]{2,1,0:T(8,128)(2,1)}) custom-call(bf16[32,320]{1,0:T(8,128)(2,1)} %bitcast.24, f32[32,320]{1,0:T(8,128)} %bitcast.22, bf16[320,320]{1,0:T(8,128)(2,1)} %basis.1), custom_call_target="tpu_custom_call" | custom-call | tf_op jit(solution)/shard_map/pallas_call | solution.py:58
  2.6 11.2 %all-to-all-start = ((bf16[4,32,640]{2,1,0:T(8,128)(2,1)}), bf16[4,32,640]{2,1,0:T(8,128)(2,1)S(1)}, u32[]{:S(2)}, u32[]{:S(2)}) async-start(bf16[4,32,640]{2,1,0:T(8,128)(2,1)} %get-tuple-element.12), calls=%async_computation | async-start | bytes 327680 | tf_op jit(solution)/shard_map/all_to_all | solution.py:178
  13.7 1.1 dynamic-slice_bitcast_fusion
  14.8 0.0 copy-start
  14.8 4.0 %collective-permute-start = (bf16[4,4,2,32,256]{4,3,2,1,0:T(8,128)(2,1)S(1)}, bf16[4,4,2,32,256]{4,3,2,1,0:T(8,128)(2,1)S(1)}, u32[]{:S(2)}, u32[]{:S(2)}) collective-permute-start(bf16[4,4,2,32,256]{4,3,2,1,0:T(8,128)(2,1)S(1)} %dynamic-slice_bitcast_fusion), channel_id=1, source_target_pairs={{0,8},{8,0},{1,9},{9,1},{2,10},{10,2},{3,11},{11,3},{4,12},{12,4},... | collective-permute-start | bytes 1572872 | tf_op jit(solution)/shard_map/ppermute | solution.py:181
  18.8 7.9 %all-to-all-done = bf16[4,32,640]{2,1,0:T(8,128)(2,1)S(1)} async-done(((bf16[4,32,640]{2,1,0:T(8,128)(2,1)}), bf16[4,32,640]{2,1,0:T(8,128)(2,1)S(1)}, u32[]{:S(2)}, u32[]{:S(2)}) %all-to-all-start) | async-done | bytes 163872 | tf_op jit(solution)/shard_map/all_to_all | solution.py:178
  26.7 0.9 broadcast_in_dim.8
  27.6 4.5 %all-to-all-start.1 = ((bf16[4,128,640]{2,1,0:T(8,128)(2,1)}), bf16[4,128,640]{2,1,0:T(8,128)(2,1)S(1)}, u32[]{:S(2)}, u32[]{:S(2)}) async-start(bf16[4,128,640]{2,1,0:T(8,128)(2,1)} %broadcast_in_dim.8), calls=%async_computation.1 | async-start | bytes 1310720 | tf_op jit(solution)/shard_map/all_to_all | solution.py:169
  32.0 0.2 collective-permute-done.received
  32.2 8.6 %all-to-all-done.1 = bf16[4,128,640]{2,1,0:T(8,128)(2,1)S(1)} async-done(((bf16[4,128,640]{2,1,0:T(8,128)(2,1)}), bf16[4,128,640]{2,1,0:T(8,128)(2,1)S(1)}, u32[]{:S(2)}, u32[]{:S(2)}) %all-to-all-start.1) | async-done | bytes 655392 | tf_op jit(solution)/shard_map/all_to_all | solution.py:169
  40.8 1.9 %collective-permute-start.1 = (bf16[512,640]{1,0:T(8,128)(2,1)S(1)}, bf16[512,640]{1,0:T(8,128)(2,1)S(1)}, u32[]{:S(2)}, u32[]{:S(2)}) collective-permute-start(bf16[512,640]{1,0:T(8,128)(2,1)S(1)} %bitcast.18), channel_id=1, source_target_pairs={{0,1},{1,0},{2,3},{3,2},{4,5},{5,4},{6,7},{7,6},{8,9},{9,8},{10,11... | collective-permute-start | bytes 1966088 | tf_op jit(solution)/shard_map/ppermute | solution.py:184
  42.7 0.1 pad_add_fusion.place
  42.8 0.0 copy-done
  42.8 1.1 shard_map.77.part
  43.9 0.9 collective-permute-done.1.left
  44.8 1.1 shard_map.78
  45.9 0.0 copy-start.2
  45.9 15.7 %all_to_all.30.parts = bf16[8,160,256]{2,1,0:T(8,128)(2,1)S(1)} all-to-all(bf16[8,160,256]{2,1,0:T(8,128)(2,1)S(1)} %shard_map.78), channel_id=1, replica_groups=mesh['x'=4,'zh'=2,'za'=4,'zb'=2,'y'=4,'core'=2] {'x','zb'}, dimensions={0} | all-to-all | bytes 1310720 | tf_op jit(solution)/shard_map/all_to_all | solution.py:194
  61.6 0.0 copy-done.2
  61.6 0.1 shard_map.79
  61.7 17.2 %all-gather = bf16[400,256]{1,0:T(8,128)(2,1)S(1)} all-gather(bf16[200,256]{1,0:T(8,128)(2,1)S(1)} %get-tuple-element.16), channel_id=2, replica_groups=mesh['x'=4,'zh'=2,'za'=4,'zb'=2,'y'=4,'core'=2] {'zh'}, dimensions={0}, use_global_device_ids=true | all-gather | bytes 307200 | tf_op jit(solution)/shard_map/all_gather | solution.py:198
  78.9 1.2 shard_map.80
  80.1 12.3 %all_to_all.31.direction = bf16[8,80,256]{2,1,0:T(8,128)(2,1)S(1)} all-to-all(bf16[8,80,256]{2,1,0:T(8,128)(2,1)S(1)} %get-tuple-element.18), channel_id=1, replica_groups=mesh['x'=4,'zh'=2,'za'=4,'zb'=2,'y'=4,'core'=2] {'x','zb'}, dimensions={0} | all-to-all | bytes 655360 | tf_op jit(solution)/shard_map/all_to_all | solution.py:205
  92.4 0.9 shard_map.82
  93.3 1.9 %collective-permute-start.2 = (bf16[4,320,128]{2,1,0:T(8,128)(2,1)S(1)}, bf16[4,320,128]{2,1,0:T(8,128)(2,1)S(1)}, u32[]{:S(2)}, u32[]{:S(2)}) collective-permute-start(bf16[4,320,128]{2,1,0:T(8,128)(2,1)S(1)} %shard_map.82), channel_id=1, source_target_pairs={{0,1},{1,0},{2,3},{3,2},{4,5},{5,4},{6,7},{7,6},{8,9},{9,8},{10,11... | collective-permute-start | bytes 983048 | tf_op jit(solution)/shard_map/ppermute | solution.py:209
  95.2 0.9 shard_map.81.part
  96.2 0.0 copy-start.1
  96.2 0.7 collective-permute-done.2.other
  96.8 0.1 shard_map.83
  96.9 10.3 %all_to_all.32.parts = bf16[4,320,128]{2,1,0:T(8,128)(2,1)S(1)} all-to-all(bf16[4,320,128]{2,1,0:T(8,128)(2,1)S(1)} %shard_map.83), channel_id=1, replica_groups=mesh['x'=4,'zh'=2,'za'=4,'zb'=2,'y'=4,'core'=2] {'y'}, dimensions={0} | all-to-all | bytes 655360 | tf_op jit(solution)/shard_map/all_to_all | solution.py:212
  107.2 0.0 copy-done.1
  107.2 0.4 shard_map.84
  107.6 12.7 %all_to_all.33.parts = bf16[4,80,128]{2,1,0:T(8,128)(2,1)S(1)} all-to-all(bf16[4,80,128]{2,1,0:T(8,128)(2,1)S(1)} %shard_map.84), channel_id=1, replica_groups={{48,32,16,0},{49,33,17,1},{50,34,18,2},{51,35,19,3},{52,36,20,4},{53,37..., dimensions={0} | all-to-all | bytes 163840 | tf_op jit(solution)/shard_map/all_to_all | solution.py:214
  120.3 0.7 shard_map.85
Async XLA Ops:
  2.6 24.1 %all-to-all-start = ((bf16[4,32,640]{2,1,0:T(8,128)(2,1)}), bf16[4,32,640]{2,1,0:T(8,128)(2,1)S(1)}, u32[]{:S(2)}, u32[]{:S(2)}) async-start(bf16[4,32,640]{2,1,0:T(8,128)(2,1)} %get-tuple-element.12), calls=%async_computation | async-start | bytes 327680 | tf_op jit(solution)/shard_map/all_to_all | solution.py:178
  14.8 28.0 %copy-start = (bf16[2048,256]{1,0:T(8,128)(2,1)S(1)}, bf16[2048,256]{1,0:T(8,128)(2,1)}, u32[]{:S(2)}) copy-start(bf16[2048,256]{1,0:T(8,128)(2,1)} %param.9) | copy-start | bytes 3145732
  14.8 17.4 %collective-permute-start = (bf16[4,4,2,32,256]{4,3,2,1,0:T(8,128)(2,1)S(1)}, bf16[4,4,2,32,256]{4,3,2,1,0:T(8,128)(2,1)S(1)}, u32[]{:S(2)}, u32[]{:S(2)}) collective-permute-start(bf16[4,4,2,32,256]{4,3,2,1,0:T(8,128)(2,1)S(1)} %dynamic-slice_bitcast_fusion), channel_id=1, source_target_pairs={{0,8},{8,0},{1,9},{9,1},{2,10},{10,2},{3,11},{11,3},{4,12},{12,4},... | collective-permute-start | bytes 1572872 | tf_op jit(solution)/shard_map/ppermute | solution.py:181
  27.6 13.2 %all-to-all-start.1 = ((bf16[4,128,640]{2,1,0:T(8,128)(2,1)}), bf16[4,128,640]{2,1,0:T(8,128)(2,1)S(1)}, u32[]{:S(2)}, u32[]{:S(2)}) async-start(bf16[4,128,640]{2,1,0:T(8,128)(2,1)} %broadcast_in_dim.8), calls=%async_computation.1 | async-start | bytes 1310720 | tf_op jit(solution)/shard_map/all_to_all | solution.py:169
  40.8 4.0 %collective-permute-start.1 = (bf16[512,640]{1,0:T(8,128)(2,1)S(1)}, bf16[512,640]{1,0:T(8,128)(2,1)S(1)}, u32[]{:S(2)}, u32[]{:S(2)}) collective-permute-start(bf16[512,640]{1,0:T(8,128)(2,1)S(1)} %bitcast.18), channel_id=1, source_target_pairs={{0,1},{1,0},{2,3},{3,2},{4,5},{5,4},{6,7},{7,6},{8,9},{9,8},{10,11... | collective-permute-start | bytes 1966088 | tf_op jit(solution)/shard_map/ppermute | solution.py:184
  45.9 15.7 %copy-start.2 = (f32[40,256]{1,0:T(8,128)S(1)}, f32[40,256]{1,0:T(8,128)}, u32[]{:S(2)}) copy-start(f32[40,256]{1,0:T(8,128)} %second_moment.3) | copy-start | bytes 122884
  93.3 3.5 %collective-permute-start.2 = (bf16[4,320,128]{2,1,0:T(8,128)(2,1)S(1)}, bf16[4,320,128]{2,1,0:T(8,128)(2,1)S(1)}, u32[]{:S(2)}, u32[]{:S(2)}) collective-permute-start(bf16[4,320,128]{2,1,0:T(8,128)(2,1)S(1)} %shard_map.82), channel_id=1, source_target_pairs={{0,1},{1,0},{2,3},{3,2},{4,5},{5,4},{6,7},{7,6},{8,9},{9,8},{10,11... | collective-permute-start | bytes 983048 | tf_op jit(solution)/shard_map/ppermute | solution.py:209
  96.2 11.1 %copy-start.1 = (bf16[320,320]{1,0:T(8,128)(2,1)S(1)}, bf16[320,320]{1,0:T(8,128)(2,1)}, u32[]{:S(2)}) copy-start(bf16[320,320]{1,0:T(8,128)(2,1)} %basis.1) | copy-start | bytes 614404

commit v6 on v5

--- a/solution.py
+++ b/solution.py
@@ -13,9 +13,16 @@
 bf16 = jnp.bfloat16
 X, ZH, ZA, ZB, Y, C = 4, 2, 4, 2, 4, 2
 SWAP = [(0, 1), (1, 0)]
+ZA_ORDER = (3, 2, 1, 0)
+Y_ORDER = (3, 2, 1, 0)
+XZ_ORDER = (7, 6, 5, 4, 3, 2, 1, 0)
 VMEM = pl.BlockSpec(memory_space=pltpu.VMEM)
 HBM = pl.BlockSpec(memory_space=pltpu.HBM)
 SMEM = pl.BlockSpec(memory_space=pltpu.SMEM)
+
+
+def slot(x, pair):
+    return X * ZB - 1 - x * ZB - pair
 
 
 def dot(left, right, over_left, over_right):
@@ -75,13 +82,13 @@
 
 def kept_rows(basis, pair, core):
     return jnp.concatenate(
-        [basis[za, pair, y, core] for y in range(Y) for za in range(ZA)], axis=0
+        [basis[za, pair, y, core] for y in Y_ORDER for za in ZA_ORDER], axis=0
     )
 
 
 def received_rows(received, core):
     return jnp.concatenate(
-        [received[za, y, core] for y in range(Y) for za in range(ZA)], axis=0
+        [received[za, y, core] for y in Y_ORDER for za in ZA_ORDER], axis=0
     )
 
 
@@ -97,8 +104,8 @@
     given = part[1] + dot(left[...], received_rows(received, 1 - core), 0, 0)
     for to, total in ((pair, kept.astype(bf16)), (1 - pair, given.astype(bf16))):
         for x in range(X):
-            sent[x * ZB + to, :80] = total[x * 80 : x * 80 + 80]
-            sent[x * ZB + to, 80:] = total[320 + x * 80 : 400 + x * 80]
+            sent[slot(x, to), :80] = total[x * 80 : x * 80 + 80]
+            sent[slot(x, to), 80:] = total[320 + x * 80 : 400 + x * 80]
 
 
 def sum_kernel(parts, second_moment, total, sent):
@@ -116,7 +123,7 @@
         upper, jnp.concatenate([mine, theirs], axis=0), jnp.concatenate([theirs, mine], axis=0)
     )
     after = beta_second * before + (1.0 - beta_second) * summed[:80] * summed[:80]
-    second[...] = jnp.where(upper, after[:40], after[40:])
+    second[...] = after
     direction = (summed[80:] / (jnp.sqrt(after) + epsilon_root)).astype(bf16)
     for i in range(X * ZB):
         sent[i] = direction
@@ -124,7 +131,7 @@
 
 def back_rotate(pair, core, direction, basis, received):
     def columns(which):
-        return jnp.concatenate([direction[x * ZB + which] for x in range(X)], axis=0)
+        return jnp.concatenate([direction[slot(x, which)] for x in range(X)], axis=0)
 
     back = dot(columns(pair), kept_rows(basis, pair, core), 1, 1)
     return back + dot(columns(1 - pair), received_rows(received, core), 1, 1)
@@ -151,10 +158,13 @@
     update = dot(back, basis[...], 1, 1).astype(bf16)
     for i in range(ZA):
         block = update[i * 32 : i * 32 + 32]
-        to = ZA - 1 - i
-        sent[to, :32] = block[:, :128]
-        sent[to, 32:64] = block[:, 128:256]
-        sent[to, 64:] = jnp.concatenate([block[:16, 256:], block[16:, 256:]], axis=1)
+        sent[i, :32] = block[:, :128]
+        sent[i, 32:64] = block[:, 128:256]
+        sent[i, 64:] = jnp.concatenate([block[:16, 256:], block[16:, 256:]], axis=1)
+
+
+def copy_kernel(source, target):
+    target[...] = source[...]
 
 
 def add_kernel(parts, total):
@@ -165,21 +175,24 @@
     total[16:, 256:] = value[64:, 64:]
 
 
-def spread(values, axis, count):
-    return lax.all_to_all(
-        jnp.broadcast_to(values[None], (count,) + values.shape), axis, 0, 0
-    )
+def exchange(blocks, axis, order):
+    return lax.all_to_all(blocks, axis, 0, 0, axis_index_groups=[list(order)])
+
+
+def spread(values, axis, order):
+    return exchange(jnp.broadcast_to(values[None], (len(order),) + values.shape), axis, order)
 
 
 def per_device(grad, moment, second_moment, left_basis, right_basis):
     pair = lax.axis_index("zb")
     place = jnp.stack([lax.axis_index("core"), pair, lax.axis_index("zh")])
     momentum, left = left_stage(grad.T, moment.T, left_basis)
-    left = lax.all_to_all(left, "za", 0, 0).reshape(128, 640)
+    left = exchange(left, "za", ZA_ORDER).reshape(128, 640)
     basis = right_basis.reshape(ZA, ZB, Y, C, 32, 256)
     leaving = lax.dynamic_index_in_dim(basis, 1 - pair, 1, keepdims=False)
     received = lax.ppermute(leaving, "zb", SWAP)
-    left = spread(left, "y", Y).reshape(512, 640)
+    left = spread(left, "y", Y_ORDER).reshape(512, 640)
+    (left,) = local(copy_kernel, (((512, 640), bf16),), (left,))
     left, received = lax.optimization_barrier((left, received))
     left_other = lax.ppermute(left, "core", SWAP)
     (part,) = local(
@@ -191,27 +204,29 @@
         (place, left_other, basis, received, part),
         1,
     )
-    part = lax.all_to_all(part, ("x", "zb"), 0, 0)
+    part = exchange(part, ("x", "zb"), XZ_ORDER)
     part, sent = local(
         sum_kernel, (((160, 256), f32), ((200, 256), bf16)), (part, second_moment)
     )
     both = lax.all_gather(sent, "zh")
     second, direction = local(
         direction_kernel,
-        (((40, 256), f32), ((X * ZB, 80, 256), bf16)),
+        (((80, 256), f32), ((X * ZB, 80, 256), bf16)),
         (place, part, both, second_moment),
         1,
     )
-    direction = lax.all_to_all(direction, ("x", "zb"), 0, 0)
+    direction = exchange(direction, ("x", "zb"), XZ_ORDER)
     blocks = (((Y, 320, 128), bf16),)
     operands = (place, direction, basis, received)
     (sent,) = local(back_other_kernel, blocks, operands, 1)
     other = lax.ppermute(sent, "core", SWAP)
+    second = lax.dynamic_slice_in_dim(second, 40 * place[2], 40)
+    other, second = lax.optimization_barrier((other, second))
     (part,) = local(back_own_kernel, (((Y, 320, 128), f32),), operands, 1)
     (back,) = local(back_add_kernel, blocks, (part, other))
-    back = lax.all_to_all(back, "y", 0, 0)
+    back = exchange(back, "y", Y_ORDER)
     (update,) = local(update_kernel, (((ZA, 80, 128), bf16),), (back, left_basis))
-    update = lax.all_to_all(update, "za", 0, 0, axis_index_groups=[[3, 2, 1, 0]])
+    update = exchange(update, "za", ZA_ORDER)
     (update,) = local(add_kernel, (((32, 320), f32),), (update,))
     return (momentum.T, second, update.T)
 

time: 122 us -> 118 us (0.967)
  waiting for transfers between devices: 18.2 us -> 4.36 us
  blocking collectives: 68.2 us -> 81.9 us
  starting transfers between devices: 23.4 us -> 20.9 us
    all_to_all x4 -> x5, blocking collectives: 51 us -> 67.5 us  [exchange(): return lax.all_to_all(blocks, axis, 0, 0, axis_index_groups=[list(order)])]
    all_to_all x2 -> x1, waiting for transfers between devices: 16.5 us -> 3.43 us  [exchange(): return lax.all_to_all(blocks, axis, 0, 0, axis_index_groups=[list(order)])]
    all_gather x1, blocking collectives: 17.2 us -> 14.4 us  [per_device(): both = lax.all_gather(sent, 'zh')]
    all_to_all x2 -> x1, starting transfers between devices: 15.6 us -> 13.2 us  [exchange(): return lax.all_to_all(blocks, axis, 0, 0, axis_index_groups=[list(order)])]
    pallas_call x9 -> x10, Pallas kernels: 6.4 us -> 5.9 us  [local(): pl.pallas_call(body, out_shape=shapes, in_specs=[SMEM] * scalars + [VMEM]...]
  transfers between devices with their start and end apart: 5 -> 4, of which waited for: 5 -> 2; matrix products, arithmetic and copies ran while one was open for 2% -> 2% of each run, Pallas kernels for 2% -> 2%
where the time goes in v6:
time: 118 us
  blocking collectives  81.9 us (69%)
  starting transfers between devices  20.9 us (18%)
  Pallas kernels  7.81 us (7%)
  waiting for transfers between devices  4.36 us (4%)
  local copies, waits for them, and re-layouts  1.77 us (2%)
    all_to_all x5, blocking collectives, exchange(): return lax.all_to_all(blocks, axis, 0, 0, axis_index_groups=[list(order)])  67.5 us
    all_gather x1, blocking collectives, per_device(): both = lax.all_gather(sent, 'zh')  14.4 us
    all_to_all x1, starting transfers between devices, exchange(): return lax.all_to_all(blocks, axis, 0, 0, axis_index_groups=[list(order)])  13.2 us
    pallas_call x10, Pallas kernels, local(): pl.pallas_call(body, out_shape=shapes, in_specs=[SMEM] * scalars + [VMEM]...  5.9 us
    ppermute x1, starting transfers between devices, per_device(): received = lax.ppermute(leaving, 'zb', SWAP)  3.83 us
    all_to_all x1, waiting for transfers between devices, exchange(): return lax.all_to_all(blocks, axis, 0, 0, axis_index_groups=[list(order)])  3.43 us
  transfers between devices with their start and end apart: 4, of which 2 were waited for; matrix products, arithmetic and copies ran while one was open for 2% of the time, Pallas kernels for 2%

profile of v6, /device:TPU:6, one launch (start us, length us, event | category | flops | bytes accessed | tf_op | source)
XLA Modules:
  0.0 117.6 jit_solution(16365979894460890471)
XLA Ops:
  0.6 1.9 %shard_map.76 = (f32[32,320]{1,0:T(8,128)}, bf16[4,32,640]{2,1,0:T(8,128)(2,1)}) custom-call(bf16[32,320]{1,0:T(8,128)(2,1)} %bitcast.23, f32[32,320]{1,0:T(8,128)} %bitcast.21, bf16[320,320]{1,0:T(8,128)(2,1)} %basis.1), custom_call_target="tpu_custom_call" | custom-call | tf_op jit(solution)/shard_map/pallas_call | solution.py:65
  2.5 13.2 %all-to-all-start = ((bf16[4,32,640]{2,1,0:T(8,128)(2,1)}), bf16[4,32,640]{2,1,0:T(8,128)(2,1)S(1)}, u32[]{:S(2)}, u32[]{:S(2)}) async-start(bf16[4,32,640]{2,1,0:T(8,128)(2,1)} %get-tuple-element.14), calls=%async_computation | async-start | bytes 327680 | tf_op jit(solution)/shard_map/all_to_all | solution.py:179
  15.8 1.1 dynamic-slice_bitcast_fusion
  16.9 3.8 %collective-permute-start = (bf16[4,4,2,32,256]{4,3,2,1,0:T(8,128)(2,1)S(1)}, bf16[4,4,2,32,256]{4,3,2,1,0:T(8,128)(2,1)S(1)}, u32[]{:S(2)}, u32[]{:S(2)}) collective-permute-start(bf16[4,4,2,32,256]{4,3,2,1,0:T(8,128)(2,1)S(1)} %dynamic-slice_bitcast_fusion), channel_id=1, source_target_pairs={{0,8},{8,0},{1,9},{9,1},{2,10},{10,2},{3,11},{11,3},{4,12},{12,4},... | collective-permute-start | bytes 1572872 | tf_op jit(solution)/shard_map/ppermute | solution.py:193
  20.7 3.4 %all-to-all-done = bf16[4,32,640]{2,1,0:T(8,128)(2,1)S(1)} async-done(((bf16[4,32,640]{2,1,0:T(8,128)(2,1)}), bf16[4,32,640]{2,1,0:T(8,128)(2,1)S(1)}, u32[]{:S(2)}, u32[]{:S(2)}) %all-to-all-start) | async-done | bytes 163872 | tf_op jit(solution)/shard_map/all_to_all | solution.py:179
  24.1 0.1 broadcast_in_dim.8
  24.2 0.0 copy-start
  24.2 14.0 %all_to_all.30 = bf16[4,128,640]{2,1,0:T(8,128)(2,1)S(1)} all-to-all(bf16[4,128,640]{2,1,0:T(8,128)(2,1)S(1)} %broadcast_in_dim.8), channel_id=1, replica_groups={{6,4,2,0},{7,5,3,1},{14,12,10,8},{15,13,11,9},{22,20,18,16},{23,21,19,1..., dimensions={0} | all-to-all | bytes 1310720 | tf_op jit(solution)/shard_map/all_to_all | solution.py:179
  38.2 0.1 shard_map.77.left
  38.3 0.0 collective-permute-done.received
  38.3 1.9 %collective-permute-start.1 = (bf16[512,640]{1,0:T(8,128)(2,1)S(1)}, bf16[512,640]{1,0:T(8,128)(2,1)S(1)}, u32[]{:S(2)}, u32[]{:S(2)}) collective-permute-start(bf16[512,640]{1,0:T(8,128)(2,1)S(1)} %shard_map.77.left), channel_id=1, source_target_pairs={{0,1},{1,0},{2,3},{3,2},{4,5},{5,4},{6,7},{7,6},{8,9},{9,8},{10,11... | collective-permute-start | bytes 1966088 | tf_op jit(solution)/shard_map/ppermute | solution.py:197
  40.2 0.1 pad_add_fusion.place
  40.3 0.0 copy-done
  40.3 1.1 shard_map.78.part
  41.4 0.9 collective-permute-done.1.left
  42.3 1.1 shard_map.79
  43.4 0.0 copy-start.2
  43.4 14.6 %all_to_all.31.parts = bf16[8,160,256]{2,1,0:T(8,128)(2,1)S(1)} all-to-all(bf16[8,160,256]{2,1,0:T(8,128)(2,1)S(1)} %shard_map.79), channel_id=1, replica_groups={{392,384,264,256,136,128,8,0},{393,385,265,257,137,129,9,1},{394,386,26..., dimensions={0} | all-to-all | bytes 1310720 | tf_op jit(solution)/shard_map/all_to_all | solution.py:179
  57.9 0.0 copy-done.2
  58.0 0.1 shard_map.80
  58.0 14.4 %all-gather = bf16[400,256]{1,0:T(8,128)(2,1)S(1)} all-gather(bf16[200,256]{1,0:T(8,128)(2,1)S(1)} %get-tuple-element.18), channel_id=2, replica_groups=mesh['x'=4,'zh'=2,'za'=4,'zb'=2,'y'=4,'core'=2] {'zh'}, dimensions={0}, use_global_device_ids=true | all-gather | bytes 307200 | tf_op jit(solution)/shard_map/all_gather | solution.py:211
  72.4 0.6 shard_map.81
  73.0 14.9 %all_to_all.32.direction = bf16[8,80,256]{2,1,0:T(8,128)(2,1)S(1)} all-to-all(bf16[8,80,256]{2,1,0:T(8,128)(2,1)S(1)} %get-tuple-element.19), channel_id=1, replica_groups={{392,384,264,256,136,128,8,0},{393,385,265,257,137,129,9,1},{394,386,26..., dimensions={0} | all-to-all | bytes 655360 | tf_op jit(solution)/shard_map/all_to_all | solution.py:179
  87.9 0.9 shard_map.82
  88.8 1.9 %collective-permute-start.2 = (bf16[4,320,128]{2,1,0:T(8,128)(2,1)S(1)}, bf16[4,320,128]{2,1,0:T(8,128)(2,1)S(1)}, u32[]{:S(2)}, u32[]{:S(2)}) collective-permute-start(bf16[4,320,128]{2,1,0:T(8,128)(2,1)S(1)} %shard_map.82), channel_id=1, source_target_pairs={{0,1},{1,0},{2,3},{3,2},{4,5},{5,4},{6,7},{7,6},{8,9},{9,8},{10,11... | collective-permute-start | bytes 983048 | tf_op jit(solution)/shard_map/ppermute | solution.py:222
  90.7 0.6 constant_dynamic-slice_fusion
  91.4 0.9 shard_map.83.part
  92.3 0.0 copy-start.1
  92.3 0.0 collective-permute-done.2.other
  92.3 0.1 shard_map.84
  92.4 10.7 %all_to_all.33.parts = bf16[4,320,128]{2,1,0:T(8,128)(2,1)S(1)} all-to-all(bf16[4,320,128]{2,1,0:T(8,128)(2,1)S(1)} %shard_map.84), channel_id=1, replica_groups={{6,4,2,0},{7,5,3,1},{14,12,10,8},{15,13,11,9},{22,20,18,16},{23,21,19,1..., dimensions={0} | all-to-all | bytes 655360 | tf_op jit(solution)/shard_map/all_to_all | solution.py:179
  103.1 0.0 copy-done.1
  103.1 0.4 shard_map.85
  103.4 13.4 %all_to_all.34.parts = bf16[4,80,128]{2,1,0:T(8,128)(2,1)S(1)} all-to-all(bf16[4,80,128]{2,1,0:T(8,128)(2,1)S(1)} %shard_map.85), channel_id=1, replica_groups={{48,32,16,0},{49,33,17,1},{50,34,18,2},{51,35,19,3},{52,36,20,4},{53,37..., dimensions={0} | all-to-all | bytes 163840 | tf_op jit(solution)/shard_map/all_to_all | solution.py:179
  116.9 0.7 shard_map.86
Async XLA Ops:
  2.5 21.6 %all-to-all-start = ((bf16[4,32,640]{2,1,0:T(8,128)(2,1)}), bf16[4,32,640]{2,1,0:T(8,128)(2,1)S(1)}, u32[]{:S(2)}, u32[]{:S(2)}) async-start(bf16[4,32,640]{2,1,0:T(8,128)(2,1)} %get-tuple-element.14), calls=%async_computation | async-start | bytes 327680 | tf_op jit(solution)/shard_map/all_to_all | solution.py:179
  16.9 21.4 %collective-permute-start = (bf16[4,4,2,32,256]{4,3,2,1,0:T(8,128)(2,1)S(1)}, bf16[4,4,2,32,256]{4,3,2,1,0:T(8,128)(2,1)S(1)}, u32[]{:S(2)}, u32[]{:S(2)}) collective-permute-start(bf16[4,4,2,32,256]{4,3,2,1,0:T(8,128)(2,1)S(1)} %dynamic-slice_bitcast_fusion), channel_id=1, source_target_pairs={{0,8},{8,0},{1,9},{9,1},{2,10},{10,2},{3,11},{11,3},{4,12},{12,4},... | collective-permute-start | bytes 1572872 | tf_op jit(solution)/shard_map/ppermute | solution.py:193
  24.2 16.1 %copy-start = (bf16[2048,256]{1,0:T(8,128)(2,1)S(1)}, bf16[2048,256]{1,0:T(8,128)(2,1)}, u32[]{:S(2)}) copy-start(bf16[2048,256]{1,0:T(8,128)(2,1)} %param.9) | copy-start | bytes 3145732
  38.3 4.0 %collective-permute-start.1 = (bf16[512,640]{1,0:T(8,128)(2,1)S(1)}, bf16[512,640]{1,0:T(8,128)(2,1)S(1)}, u32[]{:S(2)}, u32[]{:S(2)}) collective-permute-start(bf16[512,640]{1,0:T(8,128)(2,1)S(1)} %shard_map.77.left), channel_id=1, source_target_pairs={{0,1},{1,0},{2,3},{3,2},{4,5},{5,4},{6,7},{7,6},{8,9},{9,8},{10,11... | collective-permute-start | bytes 1966088 | tf_op jit(solution)/shard_map/ppermute | solution.py:197
  43.4 14.6 %copy-start.2 = (f32[40,256]{1,0:T(8,128)S(1)}, f32[40,256]{1,0:T(8,128)}, u32[]{:S(2)}) copy-start(f32[40,256]{1,0:T(8,128)} %second_moment.3) | copy-start | bytes 122884
  88.8 3.5 %collective-permute-start.2 = (bf16[4,320,128]{2,1,0:T(8,128)(2,1)S(1)}, bf16[4,320,128]{2,1,0:T(8,128)(2,1)S(1)}, u32[]{:S(2)}, u32[]{:S(2)}) collective-permute-start(bf16[4,320,128]{2,1,0:T(8,128)(2,1)S(1)} %shard_map.82), channel_id=1, source_target_pairs={{0,1},{1,0},{2,3},{3,2},{4,5},{5,4},{6,7},{7,6},{8,9},{9,8},{10,11... | collective-permute-start | bytes 983048 | tf_op jit(solution)/shard_map/ppermute | solution.py:222
  92.3 10.8 %copy-start.1 = (bf16[320,320]{1,0:T(8,128)(2,1)S(1)}, bf16[320,320]{1,0:T(8,128)(2,1)}, u32[]{:S(2)}) copy-start(bf16[320,320]{1,0:T(8,128)(2,1)} %basis.1) | copy-start | bytes 614404

commit v7 on v6

--- a/solution.py
+++ b/solution.py
@@ -13,7 +13,7 @@
 bf16 = jnp.bfloat16
 X, ZH, ZA, ZB, Y, C = 4, 2, 4, 2, 4, 2
 SWAP = [(0, 1), (1, 0)]
-ZA_ORDER = (3, 2, 1, 0)
+ZA_ORDER = (2, 1, 3, 0)
 Y_ORDER = (3, 2, 1, 0)
 XZ_ORDER = (7, 6, 5, 4, 3, 2, 1, 0)
 VMEM = pl.BlockSpec(memory_space=pltpu.VMEM)

time: 118 us -> 116 us (0.983)
  starting transfers between devices: 20.9 us -> 19.4 us
    all_to_all x1, starting transfers between devices: 13.2 us -> 11.7 us  [exchange(): return lax.all_to_all(blocks, axis, 0, 0, axis_index_groups=[list(order)])]
where the time goes in v7:
time: 116 us; the launch traced here: 115 us
  blocking collectives  82.1 us (71%)
  starting transfers between devices  19.4 us (17%)
  Pallas kernels  7.82 us (7%)
  waiting for transfers between devices  3.29 us (3%)
  local copies, waits for them, and re-layouts  1.77 us (2%)
    all_to_all x5, blocking collectives, exchange(): return lax.all_to_all(blocks, axis, 0, 0, axis_index_groups=[list(order)])  67.7 us
    all_gather x1, blocking collectives, per_device(): both = lax.all_gather(sent, 'zh')  14.4 us
    all_to_all x1, starting transfers between devices, exchange(): return lax.all_to_all(blocks, axis, 0, 0, axis_index_groups=[list(order)])  11.7 us
    pallas_call x10, Pallas kernels, local(): pl.pallas_call(body, out_shape=shapes, in_specs=[SMEM] * scalars + [VMEM]...  5.91 us
    ppermute x1, starting transfers between devices, per_device(): received = lax.ppermute(leaving, 'zb', SWAP)  3.83 us
    all_to_all x1, waiting for transfers between devices, exchange(): return lax.all_to_all(blocks, axis, 0, 0, axis_index_groups=[list(order)])  2.37 us
  transfers between devices with their start and end apart: 4, of which 2 were waited for; matrix products, arithmetic and copies ran while one was open for 2% of the time, Pallas kernels for 2%

profile of v7, /device:TPU:6, one launch (start us, length us, event | category | flops | bytes accessed | tf_op | source)
XLA Modules:
  0.0 115.2 jit_solution(3657662605363294120)
XLA Ops:
  0.6 1.9 %shard_map.76 = (f32[32,320]{1,0:T(8,128)}, bf16[4,32,640]{2,1,0:T(8,128)(2,1)}) custom-call(bf16[32,320]{1,0:T(8,128)(2,1)} %bitcast.23, f32[32,320]{1,0:T(8,128)} %bitcast.21, bf16[320,320]{1,0:T(8,128)(2,1)} %basis.1), custom_call_target="tpu_custom_call" | custom-call | tf_op jit(solution)/shard_map/pallas_call | solution.py:65
  2.5 11.7 %all-to-all-start = ((bf16[4,32,640]{2,1,0:T(8,128)(2,1)}), bf16[4,32,640]{2,1,0:T(8,128)(2,1)S(1)}, u32[]{:S(2)}, u32[]{:S(2)}) async-start(bf16[4,32,640]{2,1,0:T(8,128)(2,1)} %get-tuple-element.14), calls=%async_computation | async-start | bytes 327680 | tf_op jit(solution)/shard_map/all_to_all | solution.py:179
  14.3 1.1 dynamic-slice_bitcast_fusion
  15.4 3.8 %collective-permute-start = (bf16[4,4,2,32,256]{4,3,2,1,0:T(8,128)(2,1)S(1)}, bf16[4,4,2,32,256]{4,3,2,1,0:T(8,128)(2,1)S(1)}, u32[]{:S(2)}, u32[]{:S(2)}) collective-permute-start(bf16[4,4,2,32,256]{4,3,2,1,0:T(8,128)(2,1)S(1)} %dynamic-slice_bitcast_fusion), channel_id=1, source_target_pairs={{0,8},{8,0},{1,9},{9,1},{2,10},{10,2},{3,11},{11,3},{4,12},{12,4},... | collective-permute-start | bytes 1572872 | tf_op jit(solution)/shard_map/ppermute | solution.py:193
  19.2 2.4 %all-to-all-done = bf16[4,32,640]{2,1,0:T(8,128)(2,1)S(1)} async-done(((bf16[4,32,640]{2,1,0:T(8,128)(2,1)}), bf16[4,32,640]{2,1,0:T(8,128)(2,1)S(1)}, u32[]{:S(2)}, u32[]{:S(2)}) %all-to-all-start) | async-done | bytes 163872 | tf_op jit(solution)/shard_map/all_to_all | solution.py:179
  21.6 0.1 broadcast_in_dim.8
  21.6 0.0 copy-start
  21.6 12.3 %all_to_all.30 = bf16[4,128,640]{2,1,0:T(8,128)(2,1)S(1)} all-to-all(bf16[4,128,640]{2,1,0:T(8,128)(2,1)S(1)} %broadcast_in_dim.8), channel_id=1, replica_groups={{6,4,2,0},{7,5,3,1},{14,12,10,8},{15,13,11,9},{22,20,18,16},{23,21,19,1..., dimensions={0} | all-to-all | bytes 1310720 | tf_op jit(solution)/shard_map/all_to_all | solution.py:179
  33.9 0.1 shard_map.77.left
  34.0 0.0 collective-permute-done.received
  34.0 1.9 %collective-permute-start.1 = (bf16[512,640]{1,0:T(8,128)(2,1)S(1)}, bf16[512,640]{1,0:T(8,128)(2,1)S(1)}, u32[]{:S(2)}, u32[]{:S(2)}) collective-permute-start(bf16[512,640]{1,0:T(8,128)(2,1)S(1)} %shard_map.77.left), channel_id=1, source_target_pairs={{0,1},{1,0},{2,3},{3,2},{4,5},{5,4},{6,7},{7,6},{8,9},{9,8},{10,11... | collective-permute-start | bytes 1966088 | tf_op jit(solution)/shard_map/ppermute | solution.py:197
  35.9 0.1 pad_add_fusion.place
  36.0 0.0 copy-done
  36.0 1.1 shard_map.78.part
  37.1 0.9 collective-permute-done.1.left
  38.0 1.1 shard_map.79
  39.1 0.0 copy-start.2
  39.1 15.6 %all_to_all.31.parts = bf16[8,160,256]{2,1,0:T(8,128)(2,1)S(1)} all-to-all(bf16[8,160,256]{2,1,0:T(8,128)(2,1)S(1)} %shard_map.79), channel_id=1, replica_groups={{392,384,264,256,136,128,8,0},{393,385,265,257,137,129,9,1},{394,386,26..., dimensions={0} | all-to-all | bytes 1310720 | tf_op jit(solution)/shard_map/all_to_all | solution.py:179
  54.7 0.0 copy-done.2
  54.7 0.1 shard_map.80
  54.8 14.4 %all-gather = bf16[400,256]{1,0:T(8,128)(2,1)S(1)} all-gather(bf16[200,256]{1,0:T(8,128)(2,1)S(1)} %get-tuple-element.18), channel_id=2, replica_groups=mesh['x'=4,'zh'=2,'za'=4,'zb'=2,'y'=4,'core'=2] {'zh'}, dimensions={0}, use_global_device_ids=true | all-gather | bytes 307200 | tf_op jit(solution)/shard_map/all_gather | solution.py:211
  69.1 0.6 shard_map.81
  69.7 11.1 %all_to_all.32.direction = bf16[8,80,256]{2,1,0:T(8,128)(2,1)S(1)} all-to-all(bf16[8,80,256]{2,1,0:T(8,128)(2,1)S(1)} %get-tuple-element.19), channel_id=1, replica_groups={{392,384,264,256,136,128,8,0},{393,385,265,257,137,129,9,1},{394,386,26..., dimensions={0} | all-to-all | bytes 655360 | tf_op jit(solution)/shard_map/all_to_all | solution.py:179
  80.8 0.9 shard_map.82
  81.7 1.9 %collective-permute-start.2 = (bf16[4,320,128]{2,1,0:T(8,128)(2,1)S(1)}, bf16[4,320,128]{2,1,0:T(8,128)(2,1)S(1)}, u32[]{:S(2)}, u32[]{:S(2)}) collective-permute-start(bf16[4,320,128]{2,1,0:T(8,128)(2,1)S(1)} %shard_map.82), channel_id=1, source_target_pairs={{0,1},{1,0},{2,3},{3,2},{4,5},{5,4},{6,7},{7,6},{8,9},{9,8},{10,11... | collective-permute-start | bytes 983048 | tf_op jit(solution)/shard_map/ppermute | solution.py:222
  83.6 0.6 constant_dynamic-slice_fusion
  84.3 0.9 shard_map.83.part
  85.2 0.0 copy-start.1
  85.2 0.0 collective-permute-done.2.other
  85.2 0.1 shard_map.84
  85.3 10.7 %all_to_all.33.parts = bf16[4,320,128]{2,1,0:T(8,128)(2,1)S(1)} all-to-all(bf16[4,320,128]{2,1,0:T(8,128)(2,1)S(1)} %shard_map.84), channel_id=1, replica_groups={{6,4,2,0},{7,5,3,1},{14,12,10,8},{15,13,11,9},{22,20,18,16},{23,21,19,1..., dimensions={0} | all-to-all | bytes 655360 | tf_op jit(solution)/shard_map/all_to_all | solution.py:179
  96.0 0.0 copy-done.1
  96.0 0.4 shard_map.85
  96.3 18.2 %all_to_all.34.parts = bf16[4,80,128]{2,1,0:T(8,128)(2,1)S(1)} all-to-all(bf16[4,80,128]{2,1,0:T(8,128)(2,1)S(1)} %shard_map.85), channel_id=1, replica_groups={{32,16,48,0},{33,17,49,1},{34,18,50,2},{35,19,51,3},{36,20,52,4},{37,21..., dimensions={0} | all-to-all | bytes 163840 | tf_op jit(solution)/shard_map/all_to_all | solution.py:179
  114.5 0.7 shard_map.86
Async XLA Ops:
  2.5 19.0 %all-to-all-start = ((bf16[4,32,640]{2,1,0:T(8,128)(2,1)}), bf16[4,32,640]{2,1,0:T(8,128)(2,1)S(1)}, u32[]{:S(2)}, u32[]{:S(2)}) async-start(bf16[4,32,640]{2,1,0:T(8,128)(2,1)} %get-tuple-element.14), calls=%async_computation | async-start | bytes 327680 | tf_op jit(solution)/shard_map/all_to_all | solution.py:179
  15.4 18.6 %collective-permute-start = (bf16[4,4,2,32,256]{4,3,2,1,0:T(8,128)(2,1)S(1)}, bf16[4,4,2,32,256]{4,3,2,1,0:T(8,128)(2,1)S(1)}, u32[]{:S(2)}, u32[]{:S(2)}) collective-permute-start(bf16[4,4,2,32,256]{4,3,2,1,0:T(8,128)(2,1)S(1)} %dynamic-slice_bitcast_fusion), channel_id=1, source_target_pairs={{0,8},{8,0},{1,9},{9,1},{2,10},{10,2},{3,11},{11,3},{4,12},{12,4},... | collective-permute-start | bytes 1572872 | tf_op jit(solution)/shard_map/ppermute | solution.py:193
  21.6 14.4 %copy-start = (bf16[2048,256]{1,0:T(8,128)(2,1)S(1)}, bf16[2048,256]{1,0:T(8,128)(2,1)}, u32[]{:S(2)}) copy-start(bf16[2048,256]{1,0:T(8,128)(2,1)} %param.9) | copy-start | bytes 3145732
  34.0 4.0 %collective-permute-start.1 = (bf16[512,640]{1,0:T(8,128)(2,1)S(1)}, bf16[512,640]{1,0:T(8,128)(2,1)S(1)}, u32[]{:S(2)}, u32[]{:S(2)}) collective-permute-start(bf16[512,640]{1,0:T(8,128)(2,1)S(1)} %shard_map.77.left), channel_id=1, source_target_pairs={{0,1},{1,0},{2,3},{3,2},{4,5},{5,4},{6,7},{7,6},{8,9},{9,8},{10,11... | collective-permute-start | bytes 1966088 | tf_op jit(solution)/shard_map/ppermute | solution.py:197
  39.1 15.6 %copy-start.2 = (f32[40,256]{1,0:T(8,128)S(1)}, f32[40,256]{1,0:T(8,128)}, u32[]{:S(2)}) copy-start(f32[40,256]{1,0:T(8,128)} %second_moment.3) | copy-start | bytes 122884
  81.7 3.5 %collective-permute-start.2 = (bf16[4,320,128]{2,1,0:T(8,128)(2,1)S(1)}, bf16[4,320,128]{2,1,0:T(8,128)(2,1)S(1)}, u32[]{:S(2)}, u32[]{:S(2)}) collective-permute-start(bf16[4,320,128]{2,1,0:T(8,128)(2,1)S(1)} %shard_map.82), channel_id=1, source_target_pairs={{0,1},{1,0},{2,3},{3,2},{4,5},{5,4},{6,7},{7,6},{8,9},{9,8},{10,11... | collective-permute-start | bytes 983048 | tf_op jit(solution)/shard_map/ppermute | solution.py:222
  85.2 10.8 %copy-start.1 = (bf16[320,320]{1,0:T(8,128)(2,1)S(1)}, bf16[320,320]{1,0:T(8,128)(2,1)}, u32[]{:S(2)}) copy-start(bf16[320,320]{1,0:T(8,128)(2,1)} %basis.1) | copy-start | bytes 614404

commit v8 on v7

--- a/solution.py
+++ b/solution.py
@@ -14,15 +14,16 @@
 X, ZH, ZA, ZB, Y, C = 4, 2, 4, 2, 4, 2
 SWAP = [(0, 1), (1, 0)]
 ZA_ORDER = (2, 1, 3, 0)
-Y_ORDER = (3, 2, 1, 0)
-XZ_ORDER = (7, 6, 5, 4, 3, 2, 1, 0)
+Y_ORDER = (2, 1, 3, 0)
+X_ORDER = (2, 1, 3, 0)
+XZ_ORDER = (4, 5, 2, 3, 6, 7, 0, 1)
 VMEM = pl.BlockSpec(memory_space=pltpu.VMEM)
 HBM = pl.BlockSpec(memory_space=pltpu.HBM)
 SMEM = pl.BlockSpec(memory_space=pltpu.SMEM)
 
 
 def slot(x, pair):
-    return X * ZB - 1 - x * ZB - pair
+    return X_ORDER.index(x) * ZB + pair
 
 
 def dot(left, right, over_left, over_right):

time: 116 us -> 116 us (level)
  no operation moved by 1% of the time
where the time goes in v8:
time: 116 us; the launch traced here: 115 us
  blocking collectives  81.4 us (70%)
  starting transfers between devices  19.4 us (17%)
  Pallas kernels  7.82 us (7%)
  waiting for transfers between devices  3.28 us (3%)
  local copies, waits for them, and re-layouts  1.77 us (2%)
    all_to_all x5, blocking collectives, exchange(): return lax.all_to_all(blocks, axis, 0, 0, axis_index_groups=[list(order)])  67.1 us
    all_gather x1, blocking collectives, per_device(): both = lax.all_gather(sent, 'zh')  14.3 us
    all_to_all x1, starting transfers between devices, exchange(): return lax.all_to_all(blocks, axis, 0, 0, axis_index_groups=[list(order)])  11.7 us
    pallas_call x10, Pallas kernels, local(): pl.pallas_call(body, out_shape=shapes, in_specs=[SMEM] * scalars + [VMEM]...  5.91 us
    ppermute x1, starting transfers between devices, per_device(): received = lax.ppermute(leaving, 'zb', SWAP)  3.83 us
    all_to_all x1, waiting for transfers between devices, exchange(): return lax.all_to_all(blocks, axis, 0, 0, axis_index_groups=[list(order)])  2.37 us
  transfers between devices with their start and end apart: 4, of which 2 were waited for; matrix products, arithmetic and copies ran while one was open for 2% of the time, Pallas kernels for 2%

profile of v8, /device:TPU:6, one launch (start us, length us, event | category | flops | bytes accessed | tf_op | source)
XLA Modules:
  0.0 114.5 jit_solution(16635572336630102592)
XLA Ops:
  0.6 1.9 %shard_map.76 = (f32[32,320]{1,0:T(8,128)}, bf16[4,32,640]{2,1,0:T(8,128)(2,1)}) custom-call(bf16[32,320]{1,0:T(8,128)(2,1)} %bitcast.23, f32[32,320]{1,0:T(8,128)} %bitcast.21, bf16[320,320]{1,0:T(8,128)(2,1)} %basis.1), custom_call_target="tpu_custom_call" | custom-call | tf_op jit(solution)/shard_map/pallas_call | solution.py:66
  2.5 11.7 %all-to-all-start = ((bf16[4,32,640]{2,1,0:T(8,128)(2,1)}), bf16[4,32,640]{2,1,0:T(8,128)(2,1)S(1)}, u32[]{:S(2)}, u32[]{:S(2)}) async-start(bf16[4,32,640]{2,1,0:T(8,128)(2,1)} %get-tuple-element.14), calls=%async_computation | async-start | bytes 327680 | tf_op jit(solution)/shard_map/all_to_all | solution.py:180
  14.3 1.1 dynamic-slice_bitcast_fusion
  15.4 3.8 %collective-permute-start = (bf16[4,4,2,32,256]{4,3,2,1,0:T(8,128)(2,1)S(1)}, bf16[4,4,2,32,256]{4,3,2,1,0:T(8,128)(2,1)S(1)}, u32[]{:S(2)}, u32[]{:S(2)}) collective-permute-start(bf16[4,4,2,32,256]{4,3,2,1,0:T(8,128)(2,1)S(1)} %dynamic-slice_bitcast_fusion), channel_id=1, source_target_pairs={{0,8},{8,0},{1,9},{9,1},{2,10},{10,2},{3,11},{11,3},{4,12},{12,4},... | collective-permute-start | bytes 1572872 | tf_op jit(solution)/shard_map/ppermute | solution.py:194
  19.2 2.4 %all-to-all-done = bf16[4,32,640]{2,1,0:T(8,128)(2,1)S(1)} async-done(((bf16[4,32,640]{2,1,0:T(8,128)(2,1)}), bf16[4,32,640]{2,1,0:T(8,128)(2,1)S(1)}, u32[]{:S(2)}, u32[]{:S(2)}) %all-to-all-start) | async-done | bytes 163872 | tf_op jit(solution)/shard_map/all_to_all | solution.py:180
  21.6 0.1 broadcast_in_dim.8
  21.6 0.0 copy-start
  21.6 11.2 %all_to_all.30 = bf16[4,128,640]{2,1,0:T(8,128)(2,1)S(1)} all-to-all(bf16[4,128,640]{2,1,0:T(8,128)(2,1)S(1)} %broadcast_in_dim.8), channel_id=1, replica_groups={{4,2,6,0},{5,3,7,1},{12,10,14,8},{13,11,15,9},{20,18,22,16},{21,19,23,1..., dimensions={0} | all-to-all | bytes 1310720 | tf_op jit(solution)/shard_map/all_to_all | solution.py:180
  32.8 0.1 shard_map.77.left
  32.9 0.0 collective-permute-done.received
  32.9 1.9 %collective-permute-start.1 = (bf16[512,640]{1,0:T(8,128)(2,1)S(1)}, bf16[512,640]{1,0:T(8,128)(2,1)S(1)}, u32[]{:S(2)}, u32[]{:S(2)}) collective-permute-start(bf16[512,640]{1,0:T(8,128)(2,1)S(1)} %shard_map.77.left), channel_id=1, source_target_pairs={{0,1},{1,0},{2,3},{3,2},{4,5},{5,4},{6,7},{7,6},{8,9},{9,8},{10,11... | collective-permute-start | bytes 1966088 | tf_op jit(solution)/shard_map/ppermute | solution.py:198
  34.8 0.1 pad_add_fusion.place
  34.9 0.0 copy-done
  34.9 1.1 shard_map.78.part
  36.0 0.9 collective-permute-done.1.left
  36.9 1.1 shard_map.79
  38.0 0.0 copy-start.2
  38.0 15.9 %all_to_all.31.parts = bf16[8,160,256]{2,1,0:T(8,128)(2,1)S(1)} all-to-all(bf16[8,160,256]{2,1,0:T(8,128)(2,1)S(1)} %shard_map.79), channel_id=1, replica_groups={{256,264,128,136,384,392,0,8},{257,265,129,137,385,393,1,9},{258,266,13..., dimensions={0} | all-to-all | bytes 1310720 | tf_op jit(solution)/shard_map/all_to_all | solution.py:180
  53.9 0.0 copy-done.2
  53.9 0.1 shard_map.80
  54.0 14.3 %all-gather = bf16[400,256]{1,0:T(8,128)(2,1)S(1)} all-gather(bf16[200,256]{1,0:T(8,128)(2,1)S(1)} %get-tuple-element.18), channel_id=2, replica_groups=mesh['x'=4,'zh'=2,'za'=4,'zb'=2,'y'=4,'core'=2] {'zh'}, dimensions={0}, use_global_device_ids=true | all-gather | bytes 307200 | tf_op jit(solution)/shard_map/all_gather | solution.py:212
  68.3 0.6 shard_map.81
  68.9 10.6 %all_to_all.32.direction = bf16[8,80,256]{2,1,0:T(8,128)(2,1)S(1)} all-to-all(bf16[8,80,256]{2,1,0:T(8,128)(2,1)S(1)} %get-tuple-element.19), channel_id=1, replica_groups={{256,264,128,136,384,392,0,8},{257,265,129,137,385,393,1,9},{258,266,13..., dimensions={0} | all-to-all | bytes 655360 | tf_op jit(solution)/shard_map/all_to_all | solution.py:180
  79.5 0.9 shard_map.82
  80.4 1.9 %collective-permute-start.2 = (bf16[4,320,128]{2,1,0:T(8,128)(2,1)S(1)}, bf16[4,320,128]{2,1,0:T(8,128)(2,1)S(1)}, u32[]{:S(2)}, u32[]{:S(2)}) collective-permute-start(bf16[4,320,128]{2,1,0:T(8,128)(2,1)S(1)} %shard_map.82), channel_id=1, source_target_pairs={{0,1},{1,0},{2,3},{3,2},{4,5},{5,4},{6,7},{7,6},{8,9},{9,8},{10,11... | collective-permute-start | bytes 983048 | tf_op jit(solution)/shard_map/ppermute | solution.py:223
  82.3 0.6 constant_dynamic-slice_fusion
  83.0 0.9 shard_map.83.part
  83.9 0.0 copy-start.1
  83.9 0.0 collective-permute-done.2.other
  83.9 0.1 shard_map.84
  84.0 10.5 %all_to_all.33.parts = bf16[4,320,128]{2,1,0:T(8,128)(2,1)S(1)} all-to-all(bf16[4,320,128]{2,1,0:T(8,128)(2,1)S(1)} %shard_map.84), channel_id=1, replica_groups={{4,2,6,0},{5,3,7,1},{12,10,14,8},{13,11,15,9},{20,18,22,16},{21,19,23,1..., dimensions={0} | all-to-all | bytes 655360 | tf_op jit(solution)/shard_map/all_to_all | solution.py:180
  94.5 0.0 copy-done.1
  94.5 0.4 shard_map.85
  94.9 18.9 %all_to_all.34.parts = bf16[4,80,128]{2,1,0:T(8,128)(2,1)S(1)} all-to-all(bf16[4,80,128]{2,1,0:T(8,128)(2,1)S(1)} %shard_map.85), channel_id=1, replica_groups={{32,16,48,0},{33,17,49,1},{34,18,50,2},{35,19,51,3},{36,20,52,4},{37,21..., dimensions={0} | all-to-all | bytes 163840 | tf_op jit(solution)/shard_map/all_to_all | solution.py:180
  113.8 0.7 shard_map.86
Async XLA Ops:
  2.5 19.0 %all-to-all-start = ((bf16[4,32,640]{2,1,0:T(8,128)(2,1)}), bf16[4,32,640]{2,1,0:T(8,128)(2,1)S(1)}, u32[]{:S(2)}, u32[]{:S(2)}) async-start(bf16[4,32,640]{2,1,0:T(8,128)(2,1)} %get-tuple-element.14), calls=%async_computation | async-start | bytes 327680 | tf_op jit(solution)/shard_map/all_to_all | solution.py:180
  15.4 17.5 %collective-permute-start = (bf16[4,4,2,32,256]{4,3,2,1,0:T(8,128)(2,1)S(1)}, bf16[4,4,2,32,256]{4,3,2,1,0:T(8,128)(2,1)S(1)}, u32[]{:S(2)}, u32[]{:S(2)}) collective-permute-start(bf16[4,4,2,32,256]{4,3,2,1,0:T(8,128)(2,1)S(1)} %dynamic-slice_bitcast_fusion), channel_id=1, source_target_pairs={{0,8},{8,0},{1,9},{9,1},{2,10},{10,2},{3,11},{11,3},{4,12},{12,4},... | collective-permute-start | bytes 1572872 | tf_op jit(solution)/shard_map/ppermute | solution.py:194
  21.6 13.3 %copy-start = (bf16[2048,256]{1,0:T(8,128)(2,1)S(1)}, bf16[2048,256]{1,0:T(8,128)(2,1)}, u32[]{:S(2)}) copy-start(bf16[2048,256]{1,0:T(8,128)(2,1)} %param.9) | copy-start | bytes 3145732
  32.9 4.0 %collective-permute-start.1 = (bf16[512,640]{1,0:T(8,128)(2,1)S(1)}, bf16[512,640]{1,0:T(8,128)(2,1)S(1)}, u32[]{:S(2)}, u32[]{:S(2)}) collective-permute-start(bf16[512,640]{1,0:T(8,128)(2,1)S(1)} %shard_map.77.left), channel_id=1, source_target_pairs={{0,1},{1,0},{2,3},{3,2},{4,5},{5,4},{6,7},{7,6},{8,9},{9,8},{10,11... | collective-permute-start | bytes 1966088 | tf_op jit(solution)/shard_map/ppermute | solution.py:198
  38.0 15.9 %copy-start.2 = (f32[40,256]{1,0:T(8,128)S(1)}, f32[40,256]{1,0:T(8,128)}, u32[]{:S(2)}) copy-start(f32[40,256]{1,0:T(8,128)} %second_moment.3) | copy-start | bytes 122884
  80.4 3.5 %collective-permute-start.2 = (bf16[4,320,128]{2,1,0:T(8,128)(2,1)S(1)}, bf16[4,320,128]{2,1,0:T(8,128)(2,1)S(1)}, u32[]{:S(2)}, u32[]{:S(2)}) collective-permute-start(bf16[4,320,128]{2,1,0:T(8,128)(2,1)S(1)} %shard_map.82), channel_id=1, source_target_pairs={{0,1},{1,0},{2,3},{3,2},{4,5},{5,4},{6,7},{7,6},{8,9},{9,8},{10,11... | collective-permute-start | bytes 983048 | tf_op jit(solution)/shard_map/ppermute | solution.py:223
  83.9 10.6 %copy-start.1 = (bf16[320,320]{1,0:T(8,128)(2,1)S(1)}, bf16[320,320]{1,0:T(8,128)(2,1)}, u32[]{:S(2)}) copy-start(bf16[320,320]{1,0:T(8,128)(2,1)} %basis.1) | copy-start | bytes 614404
